TPU v7x, 128 devices: a whole 4x4x4 slice. The times are simulated.
128 devices in a mesh: tm: 4 (over y_lo, core), space: 32 (over x, y_hi, z).
Axes of the slice: x: 4, y: 4 (y_hi: 2, y_lo: 2; y = y_hi * 2 + y_lo), z: 4, core: 2. Of those that a mesh axis runs over, the one named last changes fastest.
Arguments:
- features: bfloat16 [8, 128, 128, 128], P('tm', 'space'), may hold values from -6 to 6
- weight_a: bfloat16 [3, 3, 3, 128, 256], replicated, may hold values from -0.109375 to 0.109375
- weight_b: bfloat16 [3, 3, 3, 256, 512], replicated, may hold values from -0.078125 to 0.078125
- cotangent: bfloat16 [4, 64, 64, 512], P(None, 'space', 'tm'), may hold values from -6 to 6
Outputs:
- grad_features: bfloat16 [8, 128, 128, 128], P('tm', 'space')
- grad_wa: float32 [3, 3, 3, 128, 256], P(None, None, None, None, ('tm', 'space'))
- grad_wb: float32 [3, 3, 3, 256, 512], P(None, None, None, ('tm', 'space'))
All inputs are finite; a program needn't handle non-finite values.
Results may differ from a plain program's by a relative error of at most 0.0075.
Values may be sent and summed in bfloat16 or wider, within the bound.
A program may use at most 128 MiB of HBM per device.

v0:
```python
import jax
import jax.numpy as jnp
from jax import lax
from jax.sharding import PartitionSpec as P


def with_halo(value, sides, width):
    for axis, dim in sides:
        peers, length = (lax.axis_size(axis), value.shape[dim])
        up = [(i, (i + 1) % peers) for i in range(peers - 1)]
        down = [(j, i) for i, j in up]
        last = lax.slice_in_dim(value, length - width, length, axis=dim)
        first = lax.slice_in_dim(value, 0, width, axis=dim)
        before = lax.ppermute(last, axis, up)
        after = lax.ppermute(first, axis, down)
        value = jnp.concatenate([before, value, after], axis=dim)
    return value


def conv_valid(padded, weight):
    result = lax.conv_general_dilated(
        padded[None],
        weight,
        (1, 1, 1),
        "VALID",
        dimension_numbers=("NDHWC", "DHWIO", "NDHWC"),
        preferred_element_type=jnp.float32,
    )
    return result[0]


def flipped(weight):
    return jnp.swapaxes(weight[::-1, ::-1, ::-1], 3, 4)


def weight_grad(padded, grad):
    frames, height, width = (grad.shape[0], grad.shape[1], grad.shape[2])
    pieces = []
    for offset_t in range(3):
        for offset_h in range(3):
            for offset_w in range(3):
                pieces.append(
                    padded[
                        offset_t : offset_t + frames,
                        offset_h : offset_h + height,
                        offset_w : offset_w + width,
                        :,
                    ]
                )
    stacked = jnp.concatenate(pieces, axis=3)
    total = lax.dot_general(
        stacked, grad, (((0, 1, 2), (0, 1, 2)), ((), ())), preferred_element_type=jnp.float32
    )
    return total.reshape(3, 3, 3, padded.shape[3], grad.shape[3])


def pad_width(field):
    return jnp.pad(field, ((0, 0), (0, 0), (1, 1), (0, 0)))


def pad_frames(field):
    return jnp.pad(field, ((1, 1), (0, 0), (0, 0), (0, 0)))


def shards(features, weight_a, weight_b, cotangent):
    feat_padded = pad_width(with_halo(features, (("tm", 0), ("space", 1)), 1))
    preact = conv_valid(feat_padded, weight_a)
    sigmoid_pre = jax.nn.sigmoid(preact)
    activated = preact * sigmoid_pre
    frames, height, width, channels = activated.shape
    pooled_slab = activated.reshape(frames // 2, 2, height // 2, 2, width // 2, 2, channels).mean(
        axis=(1, 3, 5)
    )
    pooled_slab = pooled_slab.astype(jnp.bfloat16)
    pooled_tile = lax.all_to_all(pooled_slab, "tm", split_axis=2, concat_axis=0, tiled=True)
    cot_padded = pad_frames(with_halo(cotangent, (("space", 1), ("tm", 2)), 1))
    pooled_padded = pad_frames(with_halo(pooled_tile, (("space", 1), ("tm", 2)), 1))
    grad_wb = lax.psum_scatter(
        weight_grad(pooled_padded, cotangent), ("tm", "space"), scatter_dimension=3, tiled=True
    )
    grad_pooled_tile = conv_valid(cot_padded, flipped(weight_b)).astype(jnp.bfloat16)
    grad_pooled = lax.all_to_all(grad_pooled_tile, "tm", split_axis=0, concat_axis=2, tiled=True)
    small = grad_pooled.astype(jnp.float32)
    upsampled = jnp.broadcast_to(
        small[:, None, :, None, :, None, :],
        (frames // 2, 2, height // 2, 2, width // 2, 2, channels),
    )
    upsampled = upsampled.reshape(frames, height, width, channels) / 8.0
    grad_pre = (upsampled * sigmoid_pre * (1.0 + preact * (1.0 - sigmoid_pre))).astype(jnp.bfloat16)
    grad_wa = lax.psum_scatter(
        weight_grad(feat_padded, grad_pre), ("tm", "space"), scatter_dimension=4, tiled=True
    )
    grad_padded = pad_width(with_halo(grad_pre, (("tm", 0), ("space", 1)), 1))
    grad_features = conv_valid(grad_padded, flipped(weight_a)).astype(jnp.bfloat16)
    return (grad_features, grad_wa, grad_wb)


def solution(mesh):
    placed = (P("tm", "space", None, None), P(), P(), P(None, "space", "tm", None))
    return jax.shard_map(
        shards,
        mesh=mesh,
        in_specs=placed,
        out_specs=(
            P("tm", "space", None, None),
            P(None, None, None, None, ("tm", "space")),
            P(None, None, None, ("tm", "space"), None),
        ),
        check_vma=False,
    )
```

profile of v0, /device:TPU:1, one launch (start us, length us, event | category | flops | bytes accessed | tf_op | source)
XLA Modules:
  0.0 366.8 jit_solution(10592288965370623129)
XLA Ops:
  8.2 4.4 %collective-permute-start = (bf16[4,1,16,512]{3,2,1,0:T(8,128)(2,1)S(1)}, bf16[4,1,16,512]{3,2,1,0:T(8,128)(2,1)S(1)}, u32[]{:S(2)}, u32[]{:S(2)}) collective-permute-start(bf16[4,1,16,512]{3,2,1,0:T(8,128)(2,1)S(1)} %get-tuple-element.31), channel_id=1, source_target_pairs={{0,1},{1,2},{2,3},{3,4},{4,5},{5,6},{6,7},{7,8},{8,9},{9,10},{10,1... | collective-permute-start | bytes 196616 | tf_op jit(solution)/shard_map/ppermute | solution.py:14
  12.6 1.3 collective-permute-start.1
  13.9 1.1 copy.42
  16.0 1.7 collective-permute-done.1
  17.8 3.8 %collective-permute-start.3 = (bf16[4,4,1,512]{3,2,1,0:T(2,128)(2,1)S(1)}, bf16[4,4,1,512]{3,2,1,0:T(2,128)(2,1)S(1)}, u32[]{:S(2)}, u32[]{:S(2)}) collective-permute-start(bf16[4,4,1,512]{3,2,1,0:T(2,128)(2,1)S(1)} %get-tuple-element.23), channel_id=1, source_target_pairs={{32,0},{64,32},{96,64},{33,1},{65,33},{97,65},{34,2},{66,34},{98,6... | collective-permute-start | bytes 49160 | tf_op jit(solution)/shard_map/ppermute | solution.py:15
  21.7 3.1 collective-permute-start.2
  25.5 1.9 collective-permute-start.5
  27.4 3.6 collective-permute-start.4
  32.0 5.5 %fusion.35 = bf16[4,2,8,3,256]{4,2,3,1,0:T(8,128)(2,1)S(1)} fusion(bf16[3,3,3,256,512]{4,3,2,1,0:T(8,128)(2,1)} %param.6, bf16[6,4,1,7,2,512]{5,3,4,1,0,2:T(8,128)(2,1)S(1)} %slice.325, bf16[6,4,1,8,3,512]{5,3,4,1,0,2:T(8,128)(2,1)S(1)} %copy.38, pred[8,3]{0,1:T(4,128)(4,1)S(1)} %copy-done.14), kind=kOutput, calls=%fused_computation.43 | convolution fusion | flops 1362001920 | bytes 8110104 | tf_op jit(solution)/shard_map/conv_general_dilated | solution.py:21
  38.2 3.3 all-to-all-start
  42.2 1.3 collective-permute-start.7
  43.5 4.8 %collective-permute-start.6 = (bf16[4,1,128,128]{2,3,1,0:T(8,128)(2,1)}, bf16[4,1,128,128]{2,3,1,0:T(8,128)(2,1)}, u32[]{:S(2)}, u32[]{:S(2)}) collective-permute-start(bf16[4,1,128,128]{2,3,1,0:T(8,128)(2,1)} %get-tuple-element.20), channel_id=1, source_target_pairs={{0,1},{1,2},{2,3},{3,4},{4,5},{5,6},{6,7},{7,8},{8,9},{9,10},{10,1... | collective-permute-start | bytes 393224 | tf_op jit(solution)/shard_map/ppermute | solution.py:14
  48.9 1.1 copy.41
  50.7 3.2 fusion.91
  53.9 3.4 copy.78
  57.3 1.5 pad.22.clone
  59.7 2.3 select_maximum_fusion.2
  62.0 1.0 pad_maximum_fusion.1
  65.6 3.3 fusion.78
  69.0 1.5 copy.58
  70.5 1.5 copy.57
  73.5 2.2 reduce_sum.14
  75.7 1.5 reduce_sum.18
  77.9 3.3 all-to-all-start.1
  81.3 2.8 fusion.57
  84.1 1.7 slice_dynamic-update-slice_fusion.1
  85.8 1.3 collective-permute-start.13
  87.1 4.5 %collective-permute-start.12 = (bf16[4,1,16,256]{3,2,1,0:T(8,128)(2,1)S(1)}, bf16[4,1,16,256]{3,2,1,0:T(8,128)(2,1)S(1)}, u32[]{:S(2)}, u32[]{:S(2)}) collective-permute-start(bf16[4,1,16,256]{3,2,1,0:T(8,128)(2,1)S(1)} %get-tuple-element.32), channel_id=1, source_target_pairs={{0,1},{1,2},{2,3},{3,4},{4,5},{5,6},{6,7},{7,8},{8,9},{9,10},{10,1... | collective-permute-start | bytes 98312 | tf_op jit(solution)/shard_map/ppermute | solution.py:14
  92.6 2.8 collective-permute-start.15
  95.5 3.7 %collective-permute-start.14 = (bf16[4,4,1,256]{3,2,1,0:T(2,128)(2,1)S(1)}, bf16[4,4,1,256]{3,2,1,0:T(2,128)(2,1)S(1)}, u32[]{:S(2)}, u32[]{:S(2)}) collective-permute-start(bf16[4,4,1,256]{3,2,1,0:T(2,128)(2,1)S(1)} %get-tuple-element.28), channel_id=1, source_target_pairs={{0,32},{32,64},{64,96},{1,33},{33,65},{65,97},{2,34},{34,66},{66,9... | collective-permute-start | bytes 24584 | tf_op jit(solution)/shard_map/ppermute | solution.py:14
  99.2 5.3 %fusion.11 = f32[3,3,3,128,256]{3,4,0,1,2:T(8,128)S(1)} fusion(bf16[3,3,3,128,2,4,128]{6,3,2,1,0,5,4:T(8,128)(2,1)} %bitcast.99, bf16[2,4,128,256,1,1,1]{3,1,2,0,6,5,4:T(4,128)(2,1)} %fusion.57), kind=kOutput, calls=%fused_computation.18 | convolution fusion | flops 1811939328 | bytes 11141120 | tf_op jit(solution)/shard_map/dot_general | solution.py:51
  104.4 2.1 copy.61
  107.7 7.1 %fusion.85 = f32[6912,512,1,1]{1,0,3,2:T(8,128)} fusion(bf16[4,2,16,6912]{3,2,1,0:T(8,128)(2,1)S(1)} %constant_dynamic-update-slice_fusion.4, bf16[4,2,16,512]{3,2,1,0:T(8,128)(2,1)S(1)} %copy-done.11), kind=kOutput, calls=%fused_computation.179 | convolution fusion | flops 905969664 | bytes 16056320 | tf_op jit(solution)/shard_map/dot_general | solution.py:51
  114.8 1.7 copy.48
  117.5 1.9 collective-permute-start.9
  119.5 3.6 collective-permute-start.8
  123.1 2.1 collective-permute-done.9
  125.2 1.2 collective-permute-done.8
  127.9 1.7 fusion.79
  129.7 1.3 collective-permute-start.11
  131.0 6.4 %collective-permute-start.10 = (bf16[4,1,128,256]{3,1,2,0:T(2,128)(2,1)}, bf16[4,1,128,256]{3,1,2,0:T(2,128)(2,1)S(1)}, u32[]{:S(2)}, u32[]{:S(2)}) collective-permute-start(bf16[4,1,128,256]{3,1,2,0:T(2,128)(2,1)} %get-tuple-element.14), channel_id=1, source_target_pairs={{0,1},{1,2},{2,3},{3,4},{4,5},{5,6},{6,7},{7,8},{8,9},{9,10},{10,1... | collective-permute-start | bytes 786440 | tf_op jit(solution)/shard_map/ppermute | solution.py:14
  137.4 10.2 %collective-permute-done.11 = bf16[4,1,128,256]{3,1,2,0:T(2,128)(2,1)S(1)} collective-permute-done((bf16[4,1,128,256]{3,1,2,0:T(2,128)(2,1)}, bf16[4,1,128,256]{3,1,2,0:T(2,128)(2,1)S(1)}, u32[]{:S(2)}, u32[]{:S(2)}) %collective-permute-start.11) | collective-permute-done | bytes 262176 | tf_op jit(solution)/shard_map/ppermute | solution.py:15
  147.6 4.1 %collective-permute-done.10 = bf16[4,1,128,256]{3,1,2,0:T(2,128)(2,1)S(1)} collective-permute-done((bf16[4,1,128,256]{3,1,2,0:T(2,128)(2,1)}, bf16[4,1,128,256]{3,1,2,0:T(2,128)(2,1)S(1)}, u32[]{:S(2)}, u32[]{:S(2)}) %collective-permute-start.10) | collective-permute-done | bytes 262176 | tf_op jit(solution)/shard_map/ppermute | solution.py:14
  151.7 2.9 fusion.5
  156.4 4.1 %fusion.31 = bf16[2,4,8,17,128]{4,2,3,1,0:T(8,128)(2,1)S(1)} fusion(bf16[3,3,3,128,256]{4,3,2,1,0:T(8,128)(2,1)S(1)} %copy-done, bf16[4,6,1,7,2,256]{5,3,4,1,0,2:T(8,128)(2,1)S(1)} %slice.335, bf16[4,6,1,8,17,256]{5,3,4,1,0,2:T(8,128)(2,1)S(1)} %copy.51, pred[8,17]{0,1:T(8,128)(4,1)S(1)} %copy-done.13), kind=kOutput, calls=%fused_computation.40 | convolution fusion | flops 1931067392 | bytes 3891336 | tf_op jit(solution)/shard_map/conv_general_dilated | solution.py:21
  161.4 195.3 %all-reduce.9.cloned.1.call-done = (f32[3,3,3,128,256]{3,4,2,1,0:T(8,128)}, f32[3,3,3,256,512]{4,3,2,1,0:T(8,128)}) async-done(((f32[3,3,3,128,256]{3,4,2,1,0:T(8,128)}, f32[3,3,3,256,512]{4,3,2,1,0:T(8,128)}), (f32[3,3,3,128,256]{3,4,2,1,0:T(8,128)}, f32[3,3,3,256,512]{4,3,2,1,0:T(8,128)})) %all-reduce.9.cloned.1.call-update) | async-done | bytes 17694736
  356.7 1.5 constant_dynamic-slice_fusion.1
  358.2 1.7 constant_dynamic-slice_fusion
  (136 shorter events, 18.9 us)
Async XLA Ops:
  7.2 58.4 %copy-start = (bf16[3,3,3,128,256]{4,3,2,1,0:T(8,128)(2,1)S(1)}, bf16[3,3,3,128,256]{4,3,2,1,0:T(8,128)(2,1)}, u32[]{:S(2)}) copy-start(bf16[3,3,3,128,256]{4,3,2,1,0:T(8,128)(2,1)} %param.5) | copy-start | bytes 5308420
  8.2 6.8 %collective-permute-start = (bf16[4,1,16,512]{3,2,1,0:T(8,128)(2,1)S(1)}, bf16[4,1,16,512]{3,2,1,0:T(8,128)(2,1)S(1)}, u32[]{:S(2)}, u32[]{:S(2)}) collective-permute-start(bf16[4,1,16,512]{3,2,1,0:T(8,128)(2,1)S(1)} %get-tuple-element.31), channel_id=1, source_target_pairs={{0,1},{1,2},{2,3},{3,4},{4,5},{5,6},{6,7},{7,8},{8,9},{9,10},{10,1... | collective-permute-start | bytes 196616 | tf_op jit(solution)/shard_map/ppermute | solution.py:14
  12.6 5.2 %collective-permute-start.1 = (bf16[4,1,16,512]{3,2,1,0:T(8,128)(2,1)S(1)}, bf16[4,1,16,512]{3,2,1,0:T(8,128)(2,1)S(1)}, u32[]{:S(2)}, u32[]{:S(2)}) collective-permute-start(bf16[4,1,16,512]{3,2,1,0:T(8,128)(2,1)S(1)} %get-tuple-element.30), channel_id=1, source_target_pairs={{1,0},{2,1},{3,2},{4,3},{5,4},{6,5},{7,6},{8,7},{9,8},{10,9},{11,1... | collective-permute-start | bytes 196616 | tf_op jit(solution)/shard_map/ppermute | solution.py:15
  15.0 35.7 %copy-start.1 = (bf16[2,4,128,128]{2,3,1,0:T(8,128)(2,1)}, bf16[2,4,128,128]{2,3,1,0:T(8,128)(2,1)S(1)}, u32[]{:S(2)}) copy-start(bf16[2,4,128,128]{2,3,1,0:T(8,128)(2,1)S(1)} %copy.42) | copy-start | bytes 786436
  17.8 13.2 %collective-permute-start.3 = (bf16[4,4,1,512]{3,2,1,0:T(2,128)(2,1)S(1)}, bf16[4,4,1,512]{3,2,1,0:T(2,128)(2,1)S(1)}, u32[]{:S(2)}, u32[]{:S(2)}) collective-permute-start(bf16[4,4,1,512]{3,2,1,0:T(2,128)(2,1)S(1)} %get-tuple-element.23), channel_id=1, source_target_pairs={{32,0},{64,32},{96,64},{33,1},{65,33},{97,65},{34,2},{66,34},{98,6... | collective-permute-start | bytes 49160 | tf_op jit(solution)/shard_map/ppermute | solution.py:15
  21.7 9.4 %collective-permute-start.2 = (bf16[4,4,1,512]{3,2,1,0:T(2,128)(2,1)S(1)}, bf16[4,4,1,512]{3,2,1,0:T(2,128)(2,1)S(1)}, u32[]{:S(2)}, u32[]{:S(2)}) collective-permute-start(bf16[4,4,1,512]{3,2,1,0:T(2,128)(2,1)S(1)} %get-tuple-element.22), channel_id=1, source_target_pairs={{0,32},{32,64},{64,96},{1,33},{33,65},{65,97},{2,34},{34,66},{66,9... | collective-permute-start | bytes 49160 | tf_op jit(solution)/shard_map/ppermute | solution.py:14
  25.5 16.0 %collective-permute-start.5 = (bf16[1,4,128,128]{2,3,1,0:T(8,128)(2,1)}, bf16[1,4,128,128]{2,3,1,0:T(8,128)(2,1)S(1)}, u32[]{:S(2)}, u32[]{:S(2)}) collective-permute-start(bf16[1,4,128,128]{2,3,1,0:T(8,128)(2,1)} %get-tuple-element.25), channel_id=1, source_target_pairs={{32,0},{64,32},{96,64},{33,1},{65,33},{97,65},{34,2},{66,34},{98,6... | collective-permute-start | bytes 393224 | tf_op jit(solution)/shard_map/ppermute | solution.py:15
  27.4 14.1 %collective-permute-start.4 = (bf16[1,4,128,128]{2,3,1,0:T(8,128)(2,1)}, bf16[1,4,128,128]{2,3,1,0:T(8,128)(2,1)S(1)}, u32[]{:S(2)}, u32[]{:S(2)}) collective-permute-start(bf16[1,4,128,128]{2,3,1,0:T(8,128)(2,1)} %get-tuple-element.24), channel_id=1, source_target_pairs={{0,32},{32,64},{64,96},{1,33},{33,65},{65,97},{2,34},{34,66},{66,9... | collective-permute-start | bytes 393224 | tf_op jit(solution)/shard_map/ppermute | solution.py:14
  31.3 0.7 copy-start.14
  38.2 10.1 %all-to-all-start = ((bf16[4,2,16,256]{3,1,2,0:T(2,128)(2,1)}), bf16[4,2,16,256]{3,1,2,0:T(2,128)(2,1)S(1)}, u32[]{:S(2)}, u32[]{:S(2)}) async-start(bf16[4,2,16,256]{3,1,2,0:T(2,128)(2,1)} %slice_bitcast_fusion.2), calls=%async_computation | async-start | bytes 131072 | tf_op jit(solution)/shard_map/all_to_all | solution.py:82
  41.5 9.2 %copy-start.4 = (bf16[1,4,128,128]{2,3,1,0:T(8,128)(2,1)}, bf16[1,4,128,128]{2,3,1,0:T(8,128)(2,1)S(1)}, u32[]{:S(2)}) copy-start(bf16[1,4,128,128]{2,3,1,0:T(8,128)(2,1)S(1)} %collective-permute-done.4) | copy-start | bytes 393220
  42.2 7.8 %collective-permute-start.7 = (bf16[4,1,128,128]{2,3,1,0:T(8,128)(2,1)}, bf16[4,1,128,128]{2,3,1,0:T(8,128)(2,1)S(1)}, u32[]{:S(2)}, u32[]{:S(2)}) collective-permute-start(bf16[4,1,128,128]{2,3,1,0:T(8,128)(2,1)} %get-tuple-element.21), channel_id=1, source_target_pairs={{1,0},{2,1},{3,2},{4,3},{5,4},{6,5},{7,6},{8,7},{9,8},{10,9},{11,1... | collective-permute-start | bytes 393224 | tf_op jit(solution)/shard_map/ppermute | solution.py:15
  43.5 7.1 %collective-permute-start.6 = (bf16[4,1,128,128]{2,3,1,0:T(8,128)(2,1)}, bf16[4,1,128,128]{2,3,1,0:T(8,128)(2,1)}, u32[]{:S(2)}, u32[]{:S(2)}) collective-permute-start(bf16[4,1,128,128]{2,3,1,0:T(8,128)(2,1)} %get-tuple-element.20), channel_id=1, source_target_pairs={{0,1},{1,2},{2,3},{3,4},{4,5},{5,6},{6,7},{7,8},{8,9},{9,10},{10,1... | collective-permute-start | bytes 393224 | tf_op jit(solution)/shard_map/ppermute | solution.py:14
  50.1 7.2 %copy-start.7 = (bf16[4,1,128,128]{2,3,1,0:T(8,128)(2,1)}, bf16[4,1,128,128]{2,3,1,0:T(8,128)(2,1)S(1)}, u32[]{:S(2)}) copy-start(bf16[4,1,128,128]{2,3,1,0:T(8,128)(2,1)S(1)} %collective-permute-done.7) | copy-start | bytes 393220
  57.3 1.7 copy-start.2
  57.3 1.7 copy-start.5
  58.8 0.9 copy-start.8
  63.1 1.6 copy-start.6
  65.0 0.7 copy-start.13
  65.6 3.3 copy-start.12
  77.9 7.9 %all-to-all-start.1 = ((bf16[1,2,64,256]{3,1,0,2:T(2,128)(2,1)}), bf16[1,2,64,256]{3,1,0,2:T(2,128)(2,1)S(1)}, u32[]{:S(2)}, u32[]{:S(2)}) async-start(bf16[1,2,64,256]{3,1,0,2:T(2,128)(2,1)} %fusion.68), calls=%async_computation.1 | async-start | bytes 131072 | tf_op jit(solution)/shard_map/all_to_all | solution.py:75
  81.2 275.5 %all-reduce.9.cloned.1.call-start = ((), (), s32[]{:S(2)}) async-start(), calls=%async_computation.2 | async-start | bytes 35389440
  85.8 6.7 %collective-permute-start.13 = (bf16[4,1,16,256]{3,2,1,0:T(8,128)(2,1)S(1)}, bf16[4,1,16,256]{3,2,1,0:T(8,128)(2,1)S(1)}, u32[]{:S(2)}, u32[]{:S(2)}) collective-permute-start(bf16[4,1,16,256]{3,2,1,0:T(8,128)(2,1)S(1)} %get-tuple-element.33), channel_id=1, source_target_pairs={{1,0},{2,1},{3,2},{4,3},{5,4},{6,5},{7,6},{8,7},{9,8},{10,9},{11,1... | collective-permute-start | bytes 98312 | tf_op jit(solution)/shard_map/ppermute | solution.py:15
  87.1 5.5 %collective-permute-start.12 = (bf16[4,1,16,256]{3,2,1,0:T(8,128)(2,1)S(1)}, bf16[4,1,16,256]{3,2,1,0:T(8,128)(2,1)S(1)}, u32[]{:S(2)}, u32[]{:S(2)}) collective-permute-start(bf16[4,1,16,256]{3,2,1,0:T(8,128)(2,1)S(1)} %get-tuple-element.32), channel_id=1, source_target_pairs={{0,1},{1,2},{2,3},{3,4},{4,5},{5,6},{6,7},{7,8},{8,9},{9,10},{10,1... | collective-permute-start | bytes 98312 | tf_op jit(solution)/shard_map/ppermute | solution.py:14
  92.6 13.9 %collective-permute-start.15 = (bf16[4,4,1,256]{3,2,1,0:T(2,128)(2,1)S(1)}, bf16[4,4,1,256]{3,2,1,0:T(2,128)(2,1)S(1)}, u32[]{:S(2)}, u32[]{:S(2)}) collective-permute-start(bf16[4,4,1,256]{3,2,1,0:T(2,128)(2,1)S(1)} %get-tuple-element.29), channel_id=1, source_target_pairs={{32,0},{64,32},{96,64},{33,1},{65,33},{97,65},{34,2},{66,34},{98,6... | collective-permute-start | bytes 24584 | tf_op jit(solution)/shard_map/ppermute | solution.py:15
  95.5 11.0 %collective-permute-start.14 = (bf16[4,4,1,256]{3,2,1,0:T(2,128)(2,1)S(1)}, bf16[4,4,1,256]{3,2,1,0:T(2,128)(2,1)S(1)}, u32[]{:S(2)}, u32[]{:S(2)}) collective-permute-start(bf16[4,4,1,256]{3,2,1,0:T(2,128)(2,1)S(1)} %get-tuple-element.28), channel_id=1, source_target_pairs={{0,32},{32,64},{64,96},{1,33},{33,65},{65,97},{2,34},{34,66},{66,9... | collective-permute-start | bytes 24584 | tf_op jit(solution)/shard_map/ppermute | solution.py:14
  106.8 0.9 copy-start.11
  114.8 1.8 copy-start.3
  117.5 7.7 %collective-permute-start.9 = (bf16[1,4,128,256]{3,1,2,0:T(4,128)(2,1)S(1)}, bf16[1,4,128,256]{3,1,2,0:T(4,128)(2,1)S(1)}, u32[]{:S(2)}, u32[]{:S(2)}) collective-permute-start(bf16[1,4,128,256]{3,1,2,0:T(4,128)(2,1)S(1)} %get-tuple-element.19), channel_id=1, source_target_pairs={{32,0},{64,32},{96,64},{33,1},{65,33},{97,65},{34,2},{66,34},{98,6... | collective-permute-start | bytes 786440 | tf_op jit(solution)/shard_map/ppermute | solution.py:15
  119.5 6.9 %collective-permute-start.8 = (bf16[1,4,128,256]{3,1,2,0:T(4,128)(2,1)S(1)}, bf16[1,4,128,256]{3,1,2,0:T(4,128)(2,1)S(1)}, u32[]{:S(2)}, u32[]{:S(2)}) collective-permute-start(bf16[1,4,128,256]{3,1,2,0:T(4,128)(2,1)S(1)} %get-tuple-element.18), channel_id=1, source_target_pairs={{0,32},{32,64},{64,96},{1,33},{33,65},{65,97},{2,34},{34,66},{66,9... | collective-permute-start | bytes 786440 | tf_op jit(solution)/shard_map/ppermute | solution.py:14
  125.2 1.2 copy-start.9
  126.4 0.7 copy-start.10
  129.7 17.9 %collective-permute-start.11 = (bf16[4,1,128,256]{3,1,2,0:T(2,128)(2,1)}, bf16[4,1,128,256]{3,1,2,0:T(2,128)(2,1)S(1)}, u32[]{:S(2)}, u32[]{:S(2)}) collective-permute-start(bf16[4,1,128,256]{3,1,2,0:T(2,128)(2,1)} %get-tuple-element.15), channel_id=1, source_target_pairs={{1,0},{2,1},{3,2},{4,3},{5,4},{6,5},{7,6},{8,7},{9,8},{10,9},{11,1... | collective-permute-start | bytes 786440 | tf_op jit(solution)/shard_map/ppermute | solution.py:15
  131.0 20.7 %collective-permute-start.10 = (bf16[4,1,128,256]{3,1,2,0:T(2,128)(2,1)}, bf16[4,1,128,256]{3,1,2,0:T(2,128)(2,1)S(1)}, u32[]{:S(2)}, u32[]{:S(2)}) collective-permute-start(bf16[4,1,128,256]{3,1,2,0:T(2,128)(2,1)} %get-tuple-element.14), channel_id=1, source_target_pairs={{0,1},{1,2},{2,3},{3,4},{4,5},{5,6},{6,7},{7,8},{8,9},{9,10},{10,1... | collective-permute-start | bytes 786440 | tf_op jit(solution)/shard_map/ppermute | solution.py:14
Sparse Core Ops, SparseCore 0:
  114.9 241.7 all-reduce.8
where the time goes:
time: 368 us; the launch traced here: 367 us
  waiting for transfers between devices  215 us (58%)
  starting transfers between devices  56.4 us (15%)
  local copies, waits for them, and re-layouts  36.4 us (10%)
  matrix products  25.2 us (7%)
  other arithmetic  18.4 us (5%)
  between operations  15 us (4%)
    unnamed x2, waiting for transfers between devices  195 us
    ppermute x8, starting transfers between devices, with_halo(): before = lax.ppermute(last, axis, up)  34.2 us
    unnamed x87, local copies, waits for them, and re-layouts  16.7 us
    ppermute x8, starting transfers between devices, with_halo(): after = lax.ppermute(first, axis, down)  15.6 us
    ppermute x8, waiting for transfers between devices, with_halo(): after = lax.ppermute(first, axis, down)  14 us
    conv_general_dilated x3, matrix products, conv_valid(): lax.conv_general_dilated(padded[None], weight, (1, 1, 1), 'VALID', dimens...  12.9 us
    dot_general x2, matrix products, weight_grad(): lax.dot_general(stacked, grad, (((0, 1, 2), (0, 1, 2)), ((), ())), prefer...  12.3 us
  transfers between devices with their start and end apart: 19, of which 8 were waited for; matrix products, arithmetic and copies ran while one was open for 11% of the time, Pallas kernels for 0%

commit v1 on v0

v1 whole, which is shorter than its diff:
```python
import jax
import jax.numpy as jnp
from jax import lax
from jax.experimental import pallas as pl
from jax.experimental.pallas import tpu as pltpu
from jax.sharding import PartitionSpec as P

F32 = jnp.float32
BF16 = jnp.bfloat16
MESH = pl.DeviceIdType.MESH
TM = 4
SPACE = 32
ZG = 4
DIRS = [(dt, ds) for dt in (-1, 0, 1) for ds in (-1, 0, 1) if (dt, ds) != (0, 0)]
TAPS = [(a, b, c) for a in range(3) for b in range(3) for c in range(3)]
NT = (((1,), (1,)), ((), ()))


def dot(a, b):
    return lax.dot_general(a, b, (((1,), (0,)), ((), ())), preferred_element_type=F32)


def dot_nt(a, b):
    return lax.dot_general(a, b, NT, preferred_element_type=F32)


def valid(t, s, dt, ds):
    ok = jnp.bool_(True)
    if dt == 1:
        ok = t < TM - 1
    if dt == -1:
        ok = t > 0
    if ds == 1:
        ok = jnp.logical_and(ok, s < SPACE - 1)
    if ds == -1:
        ok = jnp.logical_and(ok, s > 0)
    return ok


def source_span(d, size):
    return (0, size) if d == 0 else ((size - 1, 1) if d == 1 else (0, 1))


def landing_span(d, size):
    return (1, size) if d == 0 else ((0, 1) if d == 1 else (size + 1, 1))


def shift_rows(x, step):
    rows = x.shape[0]
    index = lax.broadcasted_iota(jnp.int32, x.shape, 0)
    if step == 1:
        return jnp.where(index == 0, 0.0, pltpu.roll(x, 1, 0))
    return jnp.where(index == rows - 1, 0.0, pltpu.roll(x, rows - 1, 0))


def fill_edges(buf, t, s):
    @pl.when(t == 0)
    def _():
        buf[1, 0] = jnp.zeros(buf.shape[2:], BF16)

    @pl.when(t == TM - 1)
    def _():
        buf[1, 3] = jnp.zeros(buf.shape[2:], BF16)

    @pl.when(s == 0)
    def _():
        for f in range(4):
            buf[1, f, 0] = jnp.zeros(buf.shape[3:], BF16)

    @pl.when(s == SPACE - 1)
    def _():
        for f in range(4):
            buf[1, f, 5] = jnp.zeros(buf.shape[3:], BF16)


def fill_shifts(buf):
    def step(k, carry):
        f, r = (k // 6, lax.rem(k, 6))
        x = buf[1, f, r].astype(F32)
        buf[0, f, r] = shift_rows(x, 1).astype(BF16)
        buf[2, f, r] = shift_rows(x, -1).astype(BF16)
        return carry

    lax.fori_loop(0, 24, step, 0)


def body(
    feat, wa_hbm, wb_hbm, cot,
    gf_out, ga_out, gb_out,
    wa, wb, xs, cs, cw, col, colh, colf, gps, gpl, pre, pool, pt, pz, gs, gt, zz, outa, outb,
    sb, rb, pxs, pxr, sa, ra, tmp, pld,
    wsem, fs, fr, hs, hr, ws, wr, qs, qr, ps, pr, gsend, grecv, bs, br, xsend, xrecv, asend, arecv,
):
    t = lax.axis_index("tm")
    s = lax.axis_index("space")
    z = lax.rem(s, ZG)
    group = s - z
    core = lax.rem(t, 2)
    pair = t // 2

    def remote(src, dst, send, recv, tt, ss):
        return pltpu.make_async_remote_copy(
            src_ref=src, dst_ref=dst, send_sem=send, recv_sem=recv, device_id=(tt, ss), device_id_type=MESH
        )

    def wait_bytes(ref, sem):
        pltpu.make_async_copy(ref, ref, sem).wait()

    load_wa = pltpu.make_async_copy(wa_hbm, wa, wsem.at[0])
    load_wb = pltpu.make_async_copy(wb_hbm, wb, wsem.at[1])
    load_wb.start()
    load_wa.start()

    def halo_copy(source, target, base, d, send, recv):
        dt, ds = DIRS[d]
        f0, fn = source_span(dt, 2)
        r0, rn = source_span(ds, 4)
        lf, _ = landing_span(dt, 2)
        lr, _ = landing_span(ds, 4)
        return remote(
            source.at[pl.ds(base + f0, fn), pl.ds(base + r0, rn)],
            target.at[pl.ds(lf, fn), pl.ds(lr, rn)],
            send.at[d], recv.at[d], t + dt, s + ds,
        )

    for d in range(8):
        @pl.when(valid(t, s, *DIRS[d]))
        def _(d=d):
            halo_copy(feat, xs.at[1], 0, d, fs, fr).start()

    def cot_row(ds):
        r0, _ = source_span(ds, 2)
        lr, _ = landing_span(ds, 2)
        k = 0 if ds == -1 else 1
        return remote(
            cot.at[:, pl.ds(r0, 1)], cs.at[1, pl.ds(1, 4), pl.ds(lr, 1)], hs.at[k], hr.at[k], t, s + ds
        )

    for ds in (-1, 1):
        @pl.when(valid(t, s, 0, ds))
        def _(ds=ds):
            cot_row(ds).start()

    tmp[...] = jnp.zeros_like(tmp)
    for f in range(4):
        for r in range(2):
            x = cot[f, r].astype(F32)
            k = f * 2 + r
            tmp[0, pl.ds(k, 1), :] = x[0:1, :]
            tmp[1, pl.ds(k, 1), :] = x[15:16, :]
    col[...] = tmp[...].astype(BF16)

    def cot_col(dt, ds):
        side = 0 if dt == 1 else 1
        k = 2 + side * 3 + ds + 1
        return remote(
            col.at[1 if dt == 1 else 0], colh.at[side, 1 - ds], hs.at[k], hr.at[k], t + dt, s + ds
        )

    for dt in (-1, 1):
        for ds in (-1, 0, 1):
            @pl.when(valid(t, s, dt, ds))
            def _(dt=dt, ds=ds):
                cot_col(dt, ds).start()

    def gather_cot(j, tt, zd):
        return remote(
            cot.at[:, :, :, pl.ds(pl.multiple_of(zd * 128, 128), 128)],
            cw.at[z, :, :, pl.ds(pl.multiple_of(t * 16, 16), 16), :],
            ws.at[0 if j % 4 == 0 else 1], wr.at[0 if j % 4 == 0 else 1], tt, group + zd,
        )

    for j in range(1, 16):
        gather_cot(j, lax.rem(t + j // 4, TM), lax.rem(z + j % 4, ZG)).start()
    keep_cot = pltpu.make_async_copy(
        cot.at[:, :, :, pl.ds(pl.multiple_of(z * 128, 128), 128)],
        cw.at[z, :, :, pl.ds(pl.multiple_of(t * 16, 16), 16), :],
        wsem.at[2],
    )
    keep_cot.start()

    for f in range(2):
        for r in range(4):
            xs[1, 1 + f, 1 + r] = feat[f, r]
    fill_edges(xs, t, s)
    fill_edges(gs, t, s)
    for c in range(3):
        cs[c, 0] = jnp.zeros(cs.shape[2:], BF16)
        cs[c, 5] = jnp.zeros(cs.shape[2:], BF16)
    for f in range(4):
        for r in range(2):
            cs[1, 1 + f, 1 + r] = cot[f, r]

    @pl.when(t == 0)
    def _():
        colh[0] = jnp.zeros(colh.shape[1:], BF16)

    @pl.when(t == TM - 1)
    def _():
        colh[1] = jnp.zeros(colh.shape[1:], BF16)

    @pl.when(s == 0)
    def _():
        for side in range(2):
            colh[side, 0] = jnp.zeros(colh.shape[2:], BF16)
        for f in range(4):
            cs[1, 1 + f, 0] = jnp.zeros(cs.shape[3:], BF16)
        pz[pl.ds(0, 4)] = jnp.zeros((4,) + pz.shape[1:], BF16)

    @pl.when(s == SPACE - 1)
    def _():
        for side in range(2):
            colh[side, 2] = jnp.zeros(colh.shape[2:], BF16)
        for f in range(4):
            cs[1, 1 + f, 3] = jnp.zeros(cs.shape[3:], BF16)

    @pl.when(group == SPACE - ZG)
    def _():
        pz[pl.ds(20, 4)] = jnp.zeros((4,) + pz.shape[1:], BF16)

    @pl.when(jnp.logical_and(group == 0, s > 0))
    def _():
        pz[pl.ds(0, 4)] = jnp.zeros((4,) + pz.shape[1:], BF16)

    for k in range(27, 32):
        outb[pl.ds(k * 64, 64), :] = jnp.zeros((64, 128), F32)
        outa[pl.ds(k * 256, 256), :] = jnp.zeros((256, 128), F32)
    for k in range(4):
        zz[k, 0] = jnp.zeros(zz.shape[2:], BF16)
        zz[k, 5] = jnp.zeros(zz.shape[2:], BF16)

    for ds in (-1, 1):
        @pl.when(valid(t, s, 0, -ds))
        def _(ds=ds):
            cot_row(ds).wait_recv()
    for dt in (-1, 1):
        for ds in (-1, 0, 1):
            @pl.when(valid(t, s, -dt, -ds))
            def _(dt=dt, ds=ds):
                cot_col(dt, ds).wait_recv()
    colf[...] = colh[...].astype(F32)
    index = lax.broadcasted_iota(jnp.int32, (16, 512), 0)
    for f in range(4):
        for r in range(4):
            j = (0, 1, 1, 2)[r]
            k = f * 2 + (1, 0, 1, 0)[r]
            x = cs[1, 1 + f, r].astype(F32)
            left = colf[0, j, pl.ds(k, 1), :]
            right = colf[1, j, pl.ds(k, 1), :]
            cs[0, 1 + f, r] = jnp.where(index == 0, left, pltpu.roll(x, 1, 0)).astype(BF16)
            cs[2, 1 + f, r] = jnp.where(index == 15, right, pltpu.roll(x, 15, 0)).astype(BF16)
    load_wb.wait()
    acc = jnp.zeros((128, 256), F32)
    for n, (a, b, c) in enumerate(TAPS):
        lhs = cs[2 - c, pl.ds(2 - a, 4), pl.ds(2 - b, 2)].reshape(128, 512)
        acc = acc + dot_nt(lhs, wb[n])
    gps[...] = acc.reshape(4, 2, 16, 256).astype(BF16)

    def give_tile(k):
        tt = lax.rem(t + k, TM)
        return remote(
            gps.at[tt], gpl.at[:, pl.ds(pl.multiple_of(t * 16, 16), 16), :], qs.at[k - 1], qr.at[k - 1], tt, s
        )

    for k in range(1, TM):
        give_tile(k).start()
    gpl[:, pl.ds(pl.multiple_of(t * 16, 16), 16), :] = gps[t]

    for d in range(8):
        dt, ds = DIRS[d]

        @pl.when(valid(t, s, -dt, -ds))
        def _(d=d):
            halo_copy(feat, xs.at[1], 0, d, fs, fr).wait_recv()
    fill_shifts(xs)
    load_wa.wait()
    for f in range(2):
        total = jnp.zeros((512, 256), F32)
        for a in range(3):
            parts = [xs[c, f + a, pl.ds(b, 4)].reshape(512, 128) for b in range(3) for c in range(3)]
            total = total + dot(jnp.concatenate(parts, axis=1), wa[pl.ds(a * 1152, 1152), :])
        pre[pl.ds(f * 512, 512), :] = total
    for q in range(2):
        summed = jnp.zeros((128, 256), F32)
        for f in range(2):
            for r in range(2):
                rows = pl.ds((f * 4 + q * 2 + r) * 128, 128)
                p = pre[rows, :]
                sig = jax.nn.sigmoid(p)
                summed = summed + p * sig
                pre[rows, :] = sig * (1.0 + p * (1.0 - sig))
        for lane in range(2):
            pool[lane] = summed[:, lane * 128 : lane * 128 + 128]
        for lane in range(2):
            even = pool[lane, pl.ds(0, 64, stride=2), :]
            odd = pool[lane, pl.ds(1, 64, stride=2), :]
            pld[lane, pl.ds(q * 64, 64), :] = (even + odd) * 0.125
    for lane in range(2):
        turned = pld[lane].T.astype(BF16)
        pt[2 * lane] = turned[0:64]
        pt[2 * lane + 1] = turned[64:128]

    def give_pooled(tt, ss, slot, k):
        return remote(pt.at[tt], pz.at[slot * 4 + t], ps.at[k], pr.at[k], tt, ss)

    for j in range(1, 16):
        give_pooled(lax.rem(t + j // 4, TM), group + lax.rem(z + j % 4, ZG), z + 1, 0).start()
    pz[(z + 1) * 4 + t] = pt[t]

    @pl.when(jnp.logical_and(z == 0, s > 0))
    def _():
        for j in range(16):
            give_pooled(lax.rem(t + j // 4, TM), group - ZG + j % 4, 5, 1).start()

    @pl.when(jnp.logical_and(z == ZG - 1, s < SPACE - 1))
    def _():
        for j in range(16):
            give_pooled(lax.rem(t + j // 4, TM), group + ZG + j % 4, 0, 2).start()

    for k in range(1, TM):
        give_tile(k).wait_recv()
    for q in range(2):
        u = gpl[q].astype(F32) * 0.125
        for lane in range(2):
            half = u[:, lane * 128 : lane * 128 + 128]
            pool[lane, pl.ds(0, 64, stride=2), :] = half
            pool[lane, pl.ds(1, 64, stride=2), :] = half
        for f in range(2):
            for r in range(2):
                k = f * 4 + q * 2 + r
                for lane in range(2):
                    g = pool[lane] * pre[pl.ds(k * 128, 128), pl.ds(lane * 128, 128)]
                    gs[1, 1 + f, 1 + q * 2 + r, :, pl.ds(lane * 128, 128)] = g.astype(BF16)
                    gt[pl.ds(lane * 128, 128), pl.ds(k * 128, 128)] = g.T.astype(BF16)
    for d in range(8):
        @pl.when(valid(t, s, *DIRS[d]))
        def _(d=d):
            halo_copy(gs.at[1], gs.at[1], 1, d, gsend, grecv).start()

    def term(ab, carry):
        a, b = (ab // 3, lax.rem(ab, 3))
        rhs = jnp.concatenate([xs[c, pl.ds(a, 2), pl.ds(b, 4)].reshape(1024, 128) for c in range(3)], axis=1)
        res = dot(gt[...], rhs)
        for c in range(3):
            outa[pl.ds(pl.multiple_of((ab * 3 + c) * 256, 256), 256), :] = res[:, c * 128 : c * 128 + 128]
        return carry

    lax.fori_loop(0, 9, term, 0)

    def pick_a(o):
        return jnp.concatenate([outa[pl.ds(o, 32, stride=256), :], outa[pl.ds(o + 1, 32, stride=256), :]], axis=0)

    partner = t + 1 - 2 * core

    def give_pair(y):
        rows = pl.ds(y * 32, 32)
        return remote(pxs.at[rows], pxr.at[rows], xsend.at[y], xrecv.at[y], partner, s)

    for y in range(2):
        def cut(k, carry, y=y):
            pxs[y * 32 + k] = pick_a((1 - core + 2 * y) * 64 + 2 * k).astype(BF16)
            return carry

        lax.fori_loop(0, 32, cut, 0)
        give_pair(y).start()

    wait_bytes(cw.at[0, :, :, pl.ds(0, 48), :], wr.at[0])
    wait_bytes(cw.at[pl.ds(0, 3)], wr.at[1])
    keep_cot.wait()
    wait_bytes(pz.at[pl.ds(0, 15)], pr.at[0])

    @pl.when(group > 0)
    def _():
        wait_bytes(pz.at[pl.ds(0, 4)], pr.at[2])

    @pl.when(group < SPACE - ZG)
    def _():
        wait_bytes(pz.at[pl.ds(0, 4)], pr.at[1])

    lane_id = lax.broadcasted_iota(jnp.int32, (64, 128), 1)
    low = lane_id < 64
    first = lax.rem(lane_id, 64) == 0
    last = lax.rem(lane_id, 64) == 63

    def spread(k, carry):
        block, f = (k // 4, lax.rem(k, 4))
        own = pz[(block + 1) * 4 + f].astype(F32)
        before = pltpu.roll(pz[block * 4 + f].astype(F32), 64, 1)
        after = pltpu.roll(pz[(block + 2) * 4 + f].astype(F32), 64, 1)
        turned = pltpu.roll(own, 64, 1)
        rows = [jnp.where(low, before, turned), own, jnp.where(low, turned, after)]
        for b in range(3):
            x = rows[b]
            cols = [jnp.where(first, 0.0, pltpu.roll(x, 1, 1)), x, jnp.where(last, 0.0, pltpu.roll(x, 127, 1))]
            for c in range(3):
                zz[block, 1 + f, pl.ds((b * 3 + c) * 64, 64), :] = cols[c].astype(BF16)
        return carry

    lax.fori_loop(0, 16, spread, 0)
    for a in range(3):
        lhs = jnp.concatenate([zz[block, f + a] for block in range(4) for f in range(4)], axis=1)
        outb[pl.ds(a * 576, 576), :] = dot(lhs, cw[...].reshape(2048, 128))

    def share_b(j, carry):
        ss = lax.rem(s + j, SPACE)
        o = 2 * ss
        piece = jnp.concatenate([outb[pl.ds(o, 32, stride=64), :], outb[pl.ds(o + 1, 32, stride=64), :]], axis=0)
        sb[ss] = piece.astype(BF16)

        @pl.when(j > 0)
        def _():
            remote(sb.at[ss], rb.at[s], bs, br, t, ss).start()

        return carry

    lax.fori_loop(0, SPACE, share_b, 0)
    rb[s] = sb[s]

    for y in range(2):
        give_pair(y).wait_recv()
    slot = pair * 32 + s

    def share_a(j, carry):
        y = lax.rem(pair + j // 32, 2)
        ss = lax.rem(s + j, SPACE)
        tt = core + 2 * y
        k = y * 32 + ss
        sa[k] = (pick_a(tt * 64 + 2 * ss) + pxr[k].astype(F32)).astype(BF16)

        @pl.when(j > 0)
        def _():
            remote(sa.at[k], ra.at[slot], asend, arecv, tt, ss).start()

        return carry

    lax.fori_loop(0, 64, share_a, 0)
    ra[slot] = sa[slot]

    for d in range(8):
        dt, ds = DIRS[d]

        @pl.when(valid(t, s, -dt, -ds))
        def _(d=d):
            halo_copy(gs.at[1], gs.at[1], 1, d, gsend, grecv).wait_recv()
    fill_shifts(gs)
    for f in range(2):
        total = jnp.zeros((512, 128), F32)
        for a in range(3):
            for b in range(3):
                lhs = jnp.concatenate(
                    [gs[2 - c, f + 2 - a, pl.ds(2 - b, 4)].reshape(512, 256) for c in range(3)], axis=1
                )
                rhs = jnp.concatenate(
                    [wa[pl.ds(((a * 3 + b) * 3 + c) * 128, 128), :] for c in range(3)], axis=1
                )
                total = total + dot_nt(lhs, rhs)
        gf_out[f] = total.reshape(4, 128, 128).astype(BF16)

    wait_bytes(rb.at[pl.ds(0, 31)], br)
    for k in range(4):
        def add_b(g, total, k=k):
            return total + rb[g * 4 + k].astype(F32)

        gb_out[k] = lax.fori_loop(0, 8, add_b, jnp.zeros((64, 128), F32))
    wait_bytes(ra.at[pl.ds(0, 63)], arecv)
    ga_out[...] = lax.fori_loop(0, 64, lambda k, total: total + ra[k].astype(F32), jnp.zeros((64, 128), F32))

    for d in range(8):
        @pl.when(valid(t, s, *DIRS[d]))
        def _(d=d):
            halo_copy(feat, xs.at[1], 0, d, fs, fr).wait_send()
            halo_copy(gs.at[1], gs.at[1], 1, d, gsend, grecv).wait_send()
    for ds in (-1, 1):
        @pl.when(valid(t, s, 0, ds))
        def _(ds=ds):
            cot_row(ds).wait_send()
    for dt in (-1, 1):
        for ds in (-1, 0, 1):
            @pl.when(valid(t, s, dt, ds))
            def _(dt=dt, ds=ds):
                cot_col(dt, ds).wait_send()
    wait_bytes(cw.at[0, :, :, pl.ds(0, 48), :], ws.at[0])
    wait_bytes(cw.at[pl.ds(0, 3)], ws.at[1])
    for k in range(1, TM):
        give_tile(k).wait_send()
    wait_bytes(pz.at[pl.ds(0, 15)], ps.at[0])

    @pl.when(jnp.logical_and(z == 0, s > 0))
    def _():
        wait_bytes(pz.at[pl.ds(0, 16)], ps.at[1])

    @pl.when(jnp.logical_and(z == ZG - 1, s < SPACE - 1))
    def _():
        wait_bytes(pz.at[pl.ds(0, 16)], ps.at[2])

    for y in range(2):
        give_pair(y).wait_send()
    wait_bytes(rb.at[pl.ds(0, 31)], bs)
    wait_bytes(ra.at[pl.ds(0, 63)], asend)


def shards(features, weight_a, weight_b, cotangent):
    vmem = pl.BlockSpec(memory_space=pltpu.VMEM)
    far = pl.BlockSpec(memory_space=pl.ANY)
    dma = pltpu.SemaphoreType.DMA
    gf, ga, gb = pl.pallas_call(
        body,
        out_shape=(
            jax.ShapeDtypeStruct((2, 4, 128, 128), BF16),
            jax.ShapeDtypeStruct((64, 128), F32),
            jax.ShapeDtypeStruct((4, 64, 128), F32),
        ),
        in_specs=[vmem, far, far, vmem],
        out_specs=(vmem, vmem, vmem),
        scratch_shapes=[
            pltpu.VMEM((3456, 256), BF16),
            pltpu.VMEM((27, 256, 512), BF16),
            pltpu.VMEM((3, 4, 6, 128, 128), BF16),
            pltpu.VMEM((3, 6, 4, 16, 512), BF16),
            pltpu.VMEM((4, 4, 2, 64, 128), BF16),
            pltpu.VMEM((2, 16, 512), BF16),
            pltpu.VMEM((2, 3, 16, 512), BF16),
            pltpu.VMEM((2, 3, 16, 512), F32),
            pltpu.VMEM((4, 2, 16, 256), BF16),
            pltpu.VMEM((2, 64, 256), BF16),
            pltpu.VMEM((1024, 256), F32),
            pltpu.VMEM((2, 128, 128), F32),
            pltpu.VMEM((4, 64, 128), BF16),
            pltpu.VMEM((24, 64, 128), BF16),
            pltpu.VMEM((3, 4, 6, 128, 256), BF16),
            pltpu.VMEM((256, 1024), BF16),
            pltpu.VMEM((4, 6, 576, 128), BF16),
            pltpu.VMEM((8192, 128), F32),
            pltpu.VMEM((2048, 128), F32),
            pltpu.VMEM((32, 64, 128), BF16),
            pltpu.VMEM((32, 64, 128), BF16),
            pltpu.VMEM((64, 64, 128), BF16),
            pltpu.VMEM((64, 64, 128), BF16),
            pltpu.VMEM((64, 64, 128), BF16),
            pltpu.VMEM((64, 64, 128), BF16),
            pltpu.VMEM((2, 16, 512), F32),
            pltpu.VMEM((2, 128, 128), F32),
            dma((3,)), dma((8,)), dma((8,)), dma((8,)), dma((8,)), dma((2,)), dma((2,)),
            dma((3,)), dma((3,)), dma((3,)), dma((3,)), dma((8,)), dma((8,)),
            dma, dma, dma((2,)), dma((2,)), dma, dma,
        ],
        compiler_params=pltpu.CompilerParams(has_side_effects=True, vmem_limit_bytes=56 * 2**20),
    )(features, weight_a.reshape(3456, 256), weight_b.reshape(27, 256, 512), cotangent)
    grad_wa = ga.reshape(2, 32, 128)[:, :27].transpose(1, 2, 0).reshape(3, 3, 3, 128, 2)
    grad_wb = gb.reshape(4, 2, 32, 128)[:, :, :27].transpose(2, 1, 0, 3).reshape(3, 3, 3, 2, 512)
    return (gf, grad_wa, grad_wb)


def solution(mesh):
    placed = (P("tm", "space", None, None), P(), P(), P(None, "space", "tm", None))
    return jax.shard_map(
        shards,
        mesh=mesh,
        in_specs=placed,
        out_specs=(
            P("tm", "space", None, None),
            P(None, None, None, None, ("tm", "space")),
            P(None, None, None, ("tm", "space"), None),
        ),
        check_vma=False,
    )
```

time: 368 us -> 79.8 us (0.22)
  waiting for transfers between devices: 215 us -> 0 us
  Pallas kernels: 0 us -> 73.4 us
  starting transfers between devices: 56.4 us -> 0 us
  local copies, waits for them, and re-layouts: 36.4 us -> 4.78 us
  matrix products: 25.2 us -> 0 us
  other arithmetic: 18.4 us -> 0 us
  between operations: 15 us -> 0.65 us
    unnamed x2 -> x0, waiting for transfers between devices: 195 us -> none
    pallas_call x0 -> x1, Pallas kernels: none -> 73.4 us  [shards(): pl.pallas_call(body, out_shape=(jax.ShapeDtypeStruct((2, 4, 128, 128), BF...]
    ppermute x16 -> x0, starting transfers between devices: 49.8 us -> none  [the longest x8 34.2 us: with_halo(): before = lax.ppermute(last, axis, up)]
    ppermute x16 -> x0, waiting for transfers between devices: 20 us -> none  [the longest x8 14 us: with_halo(): after = lax.ppermute(first, axis, down)]
    unnamed x87 -> x1, local copies, waits for them, and re-layouts: 16.7 us -> 1.67 us
    conv_general_dilated x3 -> x0, matrix products: 12.9 us -> none  [conv_valid(): lax.conv_general_dilated(padded[None], weight, (1, 1, 1), 'VALID', dimens...]
    dot_general x2 -> x0, matrix products: 12.3 us -> none  [weight_grad(): lax.dot_general(stacked, grad, (((0, 1, 2), (0, 1, 2)), ((), ())), prefer...]
    all_to_all x2 -> x0, starting transfers between devices: 6.55 us -> none  [the longest x1 3.27 us: shards(): lax.all_to_all(pooled_slab, 'tm', split_axis=2, concat_axis=0, tiled=True)]
  transfers between devices with their start and end apart: 19 -> 0, of which waited for: 8 -> 0; matrix products, arithmetic and copies ran while one was open for 11% -> 0% of each run, Pallas kernels for 0% -> 0%
where the time goes in v1:
time: 79.8 us; the launch traced here: 78.9 us
  Pallas kernels  73.4 us (92%)
  local copies, waits for them, and re-layouts  4.78 us (6%)
    pallas_call x1, Pallas kernels, shards(): pl.pallas_call(body, out_shape=(jax.ShapeDtypeStruct((2, 4, 128, 128), BF...  73.4 us
    unnamed x1, local copies, waits for them, and re-layouts  1.67 us

profile of v1, /device:TPU:1, one launch (start us, length us, event | category | flops | bytes accessed | tf_op | source)
XLA Modules:
  0.0 78.9 jit_solution(5052143174810649028)
XLA Ops:
  0.6 73.4 %shard_map.67 = (bf16[2,4,128,128]{3,2,1,0:T(8,128)(2,1)}, f32[64,128]{1,0:T(8,128)}, f32[4,64,128]{2,1,0:T(8,128)}) custom-call(bf16[2,4,128,128]{3,2,1,0:T(8,128)(2,1)} %feat.1, bf16[3456,256]{1,0:T(8,128)(2,1)} %bitcast.10, bf16[27,256,512]{2,1,0:T(8,128)(2,1)} %bitcast.9, bf16[4,2,16,512]{3,2,1,0:T(8,128)(2,1)} %cot.1), custom_call_target="tpu_custom_call" | custom-call | tf_op jit(solution)/shard_map/pallas_call | solution.py:506
  74.1 0.9 %slice_bitcast_fusion = f32[27,2,4,128]{3,0,1,2:T(8,128)S(1)} fusion(f32[4,2,32,128]{3,2,1,0:T(8,128)} %bitcast.11), kind=kLoop, calls=%fused_computation | loop fusion | bytes 221184 | tf_op jit(solution)/shard_map/transpose | solution.py:550
  75.0 0.1 copy.8
  75.1 0.7 reshape.29
  75.8 0.8 slice_bitcast_fusion.1
  76.6 0.6 copy.7
  77.2 1.7 %copy.10 = bf16[2,4,128,128]{3,2,1,0:T(8,128)(2,1)} copy(bf16[2,4,128,128]{3,2,1,0:T(8,128)(2,1)} %get-tuple-element.12) | data formatting | bytes 524288

commit v2 on v1

v2 whole, which is shorter than its diff:
```python
import jax
import jax.numpy as jnp
from jax import lax
from jax.experimental import pallas as pl
from jax.experimental.pallas import tpu as pltpu
from jax.sharding import PartitionSpec as P

F32 = jnp.float32
BF16 = jnp.bfloat16
MESH = pl.DeviceIdType.MESH
TM = 4
SPACE = 32
ZG = 4
SIDES = [(-1, 0), (1, 0), (0, -1), (0, 1)]
CORNERS = [(dt, ds) for dt in (-1, 1) for ds in (-1, 1)]
TAPS = [(a, b, c) for a in range(3) for b in range(3) for c in range(3)]
NT = (((1,), (1,)), ((), ()))


def dot(a, b):
    return lax.dot_general(a, b, (((1,), (0,)), ((), ())), preferred_element_type=F32)


def dot_nt(a, b):
    return lax.dot_general(a, b, NT, preferred_element_type=F32)


def valid(t, s, dt, ds):
    ok = jnp.bool_(True)
    if dt == 1:
        ok = t < TM - 1
    if dt == -1:
        ok = t > 0
    if ds == 1:
        ok = jnp.logical_and(ok, s < SPACE - 1)
    if ds == -1:
        ok = jnp.logical_and(ok, s > 0)
    return ok


def source_span(d, size):
    return (0, size) if d == 0 else ((size - 1, 1) if d == 1 else (0, 1))


def landing_span(d, size):
    return (1, size) if d == 0 else ((0, 1) if d == 1 else (size + 1, 1))


def shift_rows(x, step):
    rows = x.shape[0]
    index = lax.broadcasted_iota(jnp.int32, x.shape, 0)
    if step == 1:
        return jnp.where(index == 0, 0.0, pltpu.roll(x, 1, 0))
    return jnp.where(index == rows - 1, 0.0, pltpu.roll(x, rows - 1, 0))


def fill_edges(buf, t, s):
    @pl.when(t == 0)
    def _():
        buf[1, 0] = jnp.zeros(buf.shape[2:], BF16)

    @pl.when(t == TM - 1)
    def _():
        buf[1, 3] = jnp.zeros(buf.shape[2:], BF16)

    @pl.when(s == 0)
    def _():
        for f in range(4):
            buf[1, f, 0] = jnp.zeros(buf.shape[3:], BF16)

    @pl.when(s == SPACE - 1)
    def _():
        for f in range(4):
            buf[1, f, 5] = jnp.zeros(buf.shape[3:], BF16)


def fill_shifts(buf, own):
    def shift(f, r):
        x = buf[1, f, r].astype(F32)
        buf[0, f, r] = shift_rows(x, 1).astype(BF16)
        buf[2, f, r] = shift_rows(x, -1).astype(BF16)

    def inner(k, carry):
        shift(1 + k // 4, 1 + lax.rem(k, 4))
        return carry

    def frames(k, carry):
        shift(3 * (k // 6), lax.rem(k, 6))
        return carry

    def rows(k, carry):
        shift(1 + k // 2, 5 * lax.rem(k, 2))
        return carry

    if own:
        lax.fori_loop(0, 8, inner, 0)
    else:
        lax.fori_loop(0, 12, frames, 0)
        lax.fori_loop(0, 4, rows, 0)


def body(
    feat, wa_hbm, wb_hbm, cot,
    gf_out, ga_out, gb_out,
    wa, wb, xs, cs, cw, col, colh, colf, gps, gpl, pre, pool, pt, pz, gs, gt, zz, outa, outb,
    sb, rb, pxs, pxr, su, a1, r1, t1, a2, r2, tmp, pld, edge, edges, fin, ct, ya, wt,
    wsem, fs, fr, hs, hr, ws, wr, qs, qr, ps, pr, gsend, grecv, bs, br, xsend, xrecv, asend, arecv,
):
    t = lax.axis_index("tm")
    s = lax.axis_index("space")
    z = lax.rem(s, ZG)
    group = s - z
    core = lax.rem(t, 2)
    pair = t // 2

    def remote(src, dst, send, recv, tt, ss):
        return pltpu.make_async_remote_copy(
            src_ref=src, dst_ref=dst, send_sem=send, recv_sem=recv, device_id=(tt, ss), device_id_type=MESH
        )

    def wait_bytes(ref, sem):
        pltpu.make_async_copy(ref, ref, sem).wait()

    load_wa = pltpu.make_async_copy(wa_hbm, wa, wsem.at[0])
    load_wb = pltpu.make_async_copy(wb_hbm, wb, wsem.at[1])
    keep_tile = pltpu.make_async_copy(cot, cs.at[1, pl.ds(1, 4), pl.ds(1, 2)], wsem.at[3])
    keep_feat = pltpu.make_async_copy(feat, xs.at[1, pl.ds(1, 2), pl.ds(1, 4)], wsem.at[4])
    keep_tile.start()
    keep_feat.start()
    load_wa.start()
    load_wb.start()

    barrier = pltpu.get_barrier_semaphore()

    def greet(tt, ss):
        pl.semaphore_signal(barrier, inc=1, device_id=(tt, ss), device_id_type=MESH)

    def greet_near(j, carry):
        ss = group - ZG + lax.rem(j, 12)

        @pl.when(jnp.logical_and(ss >= 0, ss < SPACE))
        def _():
            greet(1 - core + 2 * (j // 12), ss)

        return carry

    def greet_far(j, carry):
        @pl.when(j > 0)
        def _():
            greet(core + 2 * lax.rem(pair + j // 32, 2), lax.rem(s + j, SPACE))

        return carry

    lax.fori_loop(0, 24, greet_near, 0)
    lax.fori_loop(0, 64, greet_far, 0)
    greeted = 63 + 24 - jnp.where(group == 0, 8, 0) - jnp.where(group == SPACE - ZG, 8, 0)

    pl.semaphore_wait(barrier, greeted)

    lane_id = lax.broadcasted_iota(jnp.int32, (64, 128), 1)
    low = lane_id < 64
    first = lax.rem(lane_id, 64) == 0
    last = lax.rem(lane_id, 64) == 63

    def halo_copy(source, target, base, d, send, recv):
        dt, ds = SIDES[d]
        f0, fn = source_span(dt, 2)
        r0, rn = source_span(ds, 4)
        lf, _ = landing_span(dt, 2)
        lr, _ = landing_span(ds, 4)
        return remote(
            source.at[pl.ds(base + f0, fn), pl.ds(base + r0, rn)],
            target.at[pl.ds(lf, fn), pl.ds(lr, rn)],
            send.at[d], recv.at[d], t + dt, s + ds,
        )

    def halo_wait(source, target, base, ways, send, recv):
        for d in ways:
            dt, ds = SIDES[d]

            @pl.when(valid(t, s, -dt, -ds))
            def _(d=d):
                halo_copy(source, target, base, d, send, recv).wait_recv()

    def corner_copy(target, d, send, recv):
        dt, ds = CORNERS[d]
        row = pl.ds(0 if ds == 1 else 5, 1)
        return remote(
            target.at[pl.ds(2 if dt == 1 else 1, 1), row],
            target.at[pl.ds(0 if dt == 1 else 3, 1), row],
            send.at[4 + d], recv.at[4 + d], t + dt, s,
        )

    def corner_valid(d, arriving):
        dt, ds = CORNERS[d]
        return jnp.logical_and(valid(t, s, -dt if arriving else dt, 0), valid(t, s, 0, -ds))

    def corners(target, send, recv, what):
        for d in range(4):
            @pl.when(corner_valid(d, what == "recv"))
            def _(d=d):
                copy = corner_copy(target, d, send, recv)
                if what == "start":
                    copy.start()
                elif what == "recv":
                    copy.wait_recv()
                else:
                    copy.wait_send()

    for d in range(4):
        @pl.when(valid(t, s, *SIDES[d]))
        def _(d=d):
            halo_copy(feat, xs.at[1], 0, d, fs, fr).start()

    def cot_row(ds):
        r0, _ = source_span(ds, 2)
        lr, _ = landing_span(ds, 2)
        k = 0 if ds == -1 else 1
        return remote(
            cot.at[:, pl.ds(r0, 1)], cs.at[1, pl.ds(1, 4), pl.ds(lr, 1)], hs.at[k], hr.at[k], t, s + ds
        )

    for ds in (-1, 1):
        @pl.when(valid(t, s, 0, ds))
        def _(ds=ds):
            cot_row(ds).start()

    keep_tile.wait()
    tmp[...] = jnp.zeros_like(tmp)
    for f in range(4):
        for r in range(2):
            x = cs[1, 1 + f, 1 + r].astype(F32)
            k = f * 2 + r
            tmp[0, pl.ds(k, 1), :] = x[0:1, :]
            tmp[1, pl.ds(k, 1), :] = x[15:16, :]
    col[...] = tmp[...].astype(BF16)

    def cot_col(dt, ds):
        side = 0 if dt == 1 else 1
        k = 2 + side * 3 + ds + 1
        return remote(
            col.at[1 if dt == 1 else 0], colh.at[side, 1 - ds], hs.at[k], hr.at[k], t + dt, s + ds
        )

    for dt in (-1, 1):
        for ds in (-1, 0, 1):
            @pl.when(valid(t, s, dt, ds))
            def _(dt=dt, ds=ds):
                cot_col(dt, ds).start()

    def gather_cot(j, tt, zd):
        return remote(
            cot.at[:, :, :, pl.ds(pl.multiple_of(zd * 128, 128), 128)],
            cw.at[z, :, :, pl.ds(pl.multiple_of(t * 16, 16), 16), :],
            ws.at[0 if j == 4 else 1], wr.at[0 if j == 4 else 1], tt, group + zd,
        )

    for j in range(1, 8):
        gather_cot(j, core + 2 * lax.rem(pair + j // 4, 2), lax.rem(z + j % 4, ZG)).start()
    keep_cot = pltpu.make_async_copy(
        cot.at[:, :, :, pl.ds(pl.multiple_of(z * 128, 128), 128)],
        cw.at[z, :, :, pl.ds(pl.multiple_of(t * 16, 16), 16), :],
        wsem.at[2],
    )
    keep_cot.start()

    fill_edges(xs, t, s)
    fill_edges(gs, t, s)
    @pl.when(t == 0)
    def _():
        colh[0] = jnp.zeros(colh.shape[1:], BF16)

    @pl.when(t == TM - 1)
    def _():
        colh[1] = jnp.zeros(colh.shape[1:], BF16)

    @pl.when(s == 0)
    def _():
        for side in range(2):
            colh[side, 0] = jnp.zeros(colh.shape[2:], BF16)
        for f in range(4):
            cs[1, 1 + f, 0] = jnp.zeros(cs.shape[3:], BF16)

    @pl.when(s == SPACE - 1)
    def _():
        for side in range(2):
            colh[side, 2] = jnp.zeros(colh.shape[2:], BF16)
        for f in range(4):
            cs[1, 1 + f, 3] = jnp.zeros(cs.shape[3:], BF16)

    @pl.when(group == SPACE - ZG)
    def _():
        edges[1] = jnp.zeros(edges.shape[1:], BF16)

    @pl.when(group == 0)
    def _():
        edges[0] = jnp.zeros(edges.shape[1:], BF16)

    t1[...] = jnp.zeros_like(t1)
    for k in range(27, 32):
        outb[pl.ds(k * 64, 64), :] = jnp.zeros((64, 128), F32)
    for k in range(4):
        zz[k, 0] = jnp.zeros(zz.shape[2:], BF16)
        zz[k, 5] = jnp.zeros(zz.shape[2:], BF16)

    load_wa.wait()
    for n in range(27):
        wt[pl.ds(n * 256, 256), :] = wa[pl.ds(n * 128, 128), :].astype(F32).T.astype(BF16)
    keep_feat.wait()
    fill_shifts(xs, True)
    for ds in (-1, 1):
        @pl.when(valid(t, s, 0, -ds))
        def _(ds=ds):
            cot_row(ds).wait_recv()
    for dt in (-1, 1):
        for ds in (-1, 0, 1):
            @pl.when(valid(t, s, -dt, -ds))
            def _(dt=dt, ds=ds):
                cot_col(dt, ds).wait_recv()
    halo_wait(feat, xs.at[1], 0, (2, 3), fs, fr)
    corners(xs.at[1], fs, fr, "start")
    colf[...] = colh[...].astype(F32)
    index = lax.broadcasted_iota(jnp.int32, (16, 512), 0)
    for f in range(4):
        for r in range(4):
            j = (0, 1, 1, 2)[r]
            k = f * 2 + (1, 0, 1, 0)[r]
            x = cs[1, 1 + f, r].astype(F32)
            left = colf[0, j, pl.ds(k, 1), :]
            right = colf[1, j, pl.ds(k, 1), :]
            cs[0, 1 + f, r] = jnp.where(index == 0, left, pltpu.roll(x, 1, 0)).astype(BF16)
            cs[2, 1 + f, r] = jnp.where(index == 15, right, pltpu.roll(x, 15, 0)).astype(BF16)
    load_wb.wait()
    for b in range(3):
        for c in range(3):
            tile = cs[2 - c, pl.ds(1, 4), pl.ds(2 - b, 2)].reshape(128, 512)
            ct[pl.ds((b * 3 + c) * 512, 512), :] = tile.astype(F32).T.astype(BF16)
    for a in range(3):
        ya[a] = dot(jnp.concatenate([wb[a * 9 + n] for n in range(9)], axis=1), ct[...])
    cell = lax.broadcasted_iota(jnp.int32, (256, 128), 1)
    later = jnp.where(cell < 96, pltpu.roll(ya[0], 96, 1), 0.0)
    earlier = jnp.where(cell >= 32, pltpu.roll(ya[2], 32, 1), 0.0)
    gps[...] = (ya[1] + later + earlier).T.reshape(4, 2, 16, 256).astype(BF16)

    partner = t + 1 - 2 * core

    def forward_cot(y):
        part = cw.at[:, :, :, pl.ds(pl.multiple_of((core + 2 * y) * 16, 16), 16), :]
        return remote(part, part, ws.at[2 + y], wr.at[2 + y], partner, s)

    def give_tile(k):
        tt = lax.rem(t + k, TM)
        return remote(
            gps.at[tt], gpl.at[:, pl.ds(pl.multiple_of(t * 16, 16), 16), :], qs.at[k - 1], qr.at[k - 1], tt, s
        )

    for k in range(1, TM):
        give_tile(k).start()
    gpl[:, pl.ds(pl.multiple_of(t * 16, 16), 16), :] = gps[t]
    wait_bytes(cw.at[0, :, :, pl.ds(0, 16), :], wr.at[0])
    wait_bytes(cw.at[pl.ds(0, 3), :, :, pl.ds(0, 32), :], wr.at[1])
    keep_cot.wait()
    for y in range(2):
        forward_cot(y).start()

    halo_wait(feat, xs.at[1], 0, (0, 1), fs, fr)
    corners(xs.at[1], fs, fr, "recv")
    fill_shifts(xs, False)
    for f in range(2):
        parts = [xs[c, f + a, pl.ds(b, 4)].reshape(512, 128) for a, b, c in TAPS]
        pre[pl.ds(f * 512, 512), :] = dot(jnp.concatenate(parts, axis=1), wa[...])
    for q in range(2):
        summed = jnp.zeros((128, 256), F32)
        for f in range(2):
            for r in range(2):
                rows = pl.ds((f * 4 + q * 2 + r) * 128, 128)
                p = pre[rows, :]
                sig = jax.nn.sigmoid(p)
                summed = summed + p * sig
                pre[rows, :] = sig * (1.0 + p * (1.0 - sig))
        for lane in range(2):
            pool[lane] = summed[:, lane * 128 : lane * 128 + 128]
        for lane in range(2):
            even = pool[lane, pl.ds(0, 64, stride=2), :]
            odd = pool[lane, pl.ds(1, 64, stride=2), :]
            pld[lane, pl.ds(q * 64, 64), :] = (even + odd) * 0.125
    for lane in range(2):
        turned = pld[lane].astype(BF16).astype(F32).T
        for half in range(2):
            block = turned[half * 64 : half * 64 + 64]
            pt[2 * lane + half] = block.astype(BF16)
            top, bottom = (block[0:32], block[32:64])
            edge[0, 2 * lane + half] = jnp.where(low[0:32], top, pltpu.roll(bottom, 64, 1)).astype(BF16)
            edge[1, 2 * lane + half] = jnp.where(low[0:32], pltpu.roll(top, 64, 1), bottom).astype(BF16)

    def give_pooled(tt, ss):
        return remote(pt.at[tt], pz.at[(z + 1) * 4 + t], ps.at[0], pr.at[0], tt, ss)

    def give_edge(tt, ss, k):
        return remote(edge.at[k, tt], edges.at[1 - k, t], ps.at[1 + k], pr.at[2 - k], tt, ss)

    for j in range(1, 16):
        give_pooled(lax.rem(t + j // 4, TM), group + lax.rem(z + j % 4, ZG)).start()
    pz[(z + 1) * 4 + t] = pt[t]

    for k, inside, ss in ((0, jnp.logical_and(z == 0, s > 0), s - 1), (1, jnp.logical_and(z == ZG - 1, s < SPACE - 1), s + 1)):
        @pl.when(inside)
        def _(k=k, ss=ss):
            for j in range(1, TM):
                give_edge(lax.rem(t + j, TM), ss, k).start()
            give_edge(t, ss, k).start()

    for k in range(1, TM):
        give_tile(k).wait_recv()
    for q in range(2):
        u = gpl[q].astype(F32) * 0.125
        for lane in range(2):
            half = u[:, lane * 128 : lane * 128 + 128]
            pool[lane, pl.ds(0, 64, stride=2), :] = half
            pool[lane, pl.ds(1, 64, stride=2), :] = half
        for f in range(2):
            for r in range(2):
                k = f * 4 + q * 2 + r
                for lane in range(2):
                    g = pool[lane] * pre[pl.ds(k * 128, 128), pl.ds(lane * 128, 128)]
                    gs[1, 1 + f, 1 + q * 2 + r, :, pl.ds(lane * 128, 128)] = g.astype(BF16)
                    gt[pl.ds(lane * 128, 128), pl.ds(k * 128, 128)] = g.T.astype(BF16)
    for d in range(4):
        @pl.when(valid(t, s, *SIDES[d]))
        def _(d=d):
            halo_copy(gs.at[1], gs.at[1], 1, d, gsend, grecv).start()

    def pass_edge(k, zd):
        return remote(edges.at[k], edges.at[k], ps.at[3 + k], pr.at[1 + k], t, group + zd)

    for k, passes in ((0, jnp.logical_and(z == 0, s > 0)), (1, jnp.logical_and(z == ZG - 1, s < SPACE - 1))):
        @pl.when(passes)
        def _(k=k):
            wait_bytes(edges.at[k], pr.at[1 + k])
            for j in range(1, ZG):
                pass_edge(k, lax.rem(z + j, ZG)).start()


    def give_pair(m):
        taps = pl.ds(m * 9, 9)
        return remote(pxs.at[taps], pxr.at[taps], xsend.at[m], xrecv.at[m], partner, s)

    def term(ab, carry):
        a, b = (ab // 3, lax.rem(ab, 3))
        rhs = jnp.concatenate([xs[c, pl.ds(a, 2), pl.ds(b, 4)].reshape(1024, 128) for c in range(3)], axis=1)
        res = dot(gt[...], rhs)
        for c in range(3):
            n = ab * 3 + c
            base = n * 256
            outa[pl.ds(pl.multiple_of(base, 256), 256), :] = res[:, c * 128 : c * 128 + 128]
            for y in range(2):
                other = pl.multiple_of(base + (1 - core + 2 * y) * 64, 64)
                pxs[n, y] = outa[pl.ds(other, 64), :].astype(BF16)
        return carry

    for m in range(3):
        lax.fori_loop(m * 3, m * 3 + 3, term, 0)
        give_pair(m).start()
    halo_wait(gs.at[1], gs.at[1], 1, (2, 3), gsend, grecv)
    corners(gs.at[1], gsend, grecv, "start")
    fill_shifts(gs, True)

    sx, sy, sz = (s // 8, 2 * lax.rem(s // 4, 2) + pair, z)

    def place(x, y, zed):
        return (core + 2 * lax.rem(y, 2), x * 8 + (y // 2) * 4 + zed)

    coord = (sx, sy, sz)
    for m in range(3):
        give_pair(m).wait_recv()

        def add_pair(i, carry, m=m):
            n = m * 9 + i
            for y in range(2):
                own = pl.multiple_of(n * 256 + (core + 2 * y) * 64, 64)
                su[y] = outa[pl.ds(own, 64), :] + pxr[n, y].astype(F32)
            for v in range(4):
                if m == 0:
                    rows = [su[y, pl.ds(v * 16, 16), :] for y in range(2)]
                elif m == 1:
                    rows = [su[v % 2, pl.ds(x * 16 + (v // 2) * 8, 8), :] for x in range(4)]
                else:
                    rows = [su[y, pl.ds(v * 2 + e, 8, stride=8), :] for y in range(2) for e in range(2)]
                at = pl.ds(pl.multiple_of(i * 32, 32), 32)
                a1[m, v, at, :] = jnp.concatenate(rows, axis=0).astype(BF16)
            return carry

        lax.fori_loop(0, 9, add_pair, 0)
        for k in range(1, 4):
            v = lax.rem(coord[m] + k, 4)
            to = [sx, sy, sz]
            to[m] = v
            remote(a1.at[m, v], r1.at[m, coord[m]], asend.at[m], arecv.at[m], *place(*to)).start()
        r1[m, coord[m]] = a1[m, coord[m]]

    w2 = (pair * 8 + lax.rem(s, 8), sx * 4 + sz, pair * 8 + s // 4)

    def second(m):
        wait_bytes(r1.at[m, pl.ds(0, 3)], arecv.at[m])
        total = r1[m, 0].astype(F32)
        for k in range(1, 4):
            total = total + r1[m, k].astype(F32)
        t1[pl.ds(0, 288), :] = total

        def share_a(j, carry):
            d = lax.rem(w2[m] + j, 16)
            if m == 0:
                q, step, tt, ss = (d * 2, 1, core + 2 * (d // 8), sx * 8 + lax.rem(d, 8))
            elif m == 1:
                q, step, tt, ss = (d * 2, 1, t, (d // 4) * 8 + (sy // 2) * 4 + lax.rem(d, 4))
            else:
                q, step, tt, ss = ((d // 8) * 16 + lax.rem(d, 8), 8, core + 2 * (d // 8), lax.rem(d, 8) * 4 + sz)
            rows = [t1[pl.ds(q + e * step, 16, stride=32), :] for e in range(2)]
            a2[m, d] = jnp.concatenate(rows, axis=0).astype(BF16)

            @pl.when(j > 0)
            def _():
                remote(a2.at[m, d], r2.at[m, w2[m]], asend.at[3 + m], arecv.at[3 + m], tt, ss).start()

            return carry

        lax.fori_loop(0, 16, share_a, 0)
        r2[m, w2[m]] = a2[m, w2[m]]

    for y in range(2):
        forward_cot(y).wait_recv()
    wait_bytes(pz.at[pl.ds(0, 15)], pr.at[0])

    @pl.when(jnp.logical_and(group > 0, z > 0))
    def _():
        wait_bytes(edges.at[0], pr.at[1])

    @pl.when(jnp.logical_and(group < SPACE - ZG, z < ZG - 1))
    def _():
        wait_bytes(edges.at[1], pr.at[2])

    for f in range(4):
        x = edges[0, f].astype(F32)
        pz[f] = jnp.concatenate([pltpu.roll(x, 64, 1), x], axis=0).astype(BF16)
        x = edges[1, f].astype(F32)
        pz[20 + f] = jnp.concatenate([x, pltpu.roll(x, 64, 1)], axis=0).astype(BF16)

    def spread(k, carry):
        block, f = (k // 4, lax.rem(k, 4))
        own = pz[(block + 1) * 4 + f].astype(F32)
        before = pltpu.roll(pz[block * 4 + f].astype(F32), 64, 1)
        after = pltpu.roll(pz[(block + 2) * 4 + f].astype(F32), 64, 1)
        turned = pltpu.roll(own, 64, 1)
        rows = [jnp.where(low, before, turned), own, jnp.where(low, turned, after)]
        for b in range(3):
            x = rows[b]
            cols = [jnp.where(first, 0.0, pltpu.roll(x, 1, 1)), x, jnp.where(last, 0.0, pltpu.roll(x, 127, 1))]
            for c in range(3):
                zz[block, 1 + f, pl.ds((b * 3 + c) * 64, 64), :] = cols[c].astype(BF16)
        return carry

    lax.fori_loop(0, 16, spread, 0)
    for a in range(3):
        lhs = jnp.concatenate([zz[block, f + a] for block in range(4) for f in range(4)], axis=1)
        outb[pl.ds(a * 576, 576), :] = dot(lhs, cw[...].reshape(2048, 128))

    def share_b(j, carry):
        ss = lax.rem(s + j, SPACE)
        o = 2 * ss
        piece = jnp.concatenate([outb[pl.ds(o, 32, stride=64), :], outb[pl.ds(o + 1, 32, stride=64), :]], axis=0)
        sb[ss] = piece.astype(BF16)

        @pl.when(j > 0)
        def _():
            remote(sb.at[ss], rb.at[s], bs, br, t, ss).start()

        return carry

    lax.fori_loop(0, SPACE, share_b, 0)
    rb[s] = sb[s]

    for m in range(3):
        second(m)

    halo_wait(gs.at[1], gs.at[1], 1, (0, 1), gsend, grecv)
    corners(gs.at[1], gsend, grecv, "recv")
    fill_shifts(gs, False)
    for f in range(2):
        parts = [gs[2 - c, f + 2 - a, pl.ds(2 - b, 4)].reshape(512, 256) for a, b, c in TAPS]
        total = dot(jnp.concatenate(parts, axis=1), wt[...])
        gf_out[f] = total.reshape(4, 128, 128).astype(BF16)

    wait_bytes(rb.at[pl.ds(0, 31)], br)
    for k in range(4):
        def add_b(g, total, k=k):
            return total + rb[g * 4 + k].astype(F32)

        fin[...] = lax.fori_loop(0, 8, add_b, jnp.zeros((64, 128), F32))
        for n, (a, b, c) in enumerate(TAPS):
            gb_out[a, b, c, :, pl.ds(k * 128, 128)] = fin[pl.ds(n, 2, stride=32), :]
    for m in range(3):
        wait_bytes(r2.at[m, pl.ds(0, 15)], arecv.at[3 + m])

        def add_a(k, total, m=m):
            return total + r2[m, k].astype(F32)

        fin[pl.ds(0, 32), :] = lax.fori_loop(0, 16, add_a, jnp.zeros((32, 128), F32))
        for b in range(3):
            for c in range(3):
                ga_out[m, b, c] = fin[pl.ds(b * 3 + c, 2, stride=16), :]

    for d in range(4):
        @pl.when(valid(t, s, *SIDES[d]))
        def _(d=d):
            halo_copy(feat, xs.at[1], 0, d, fs, fr).wait_send()
            halo_copy(gs.at[1], gs.at[1], 1, d, gsend, grecv).wait_send()
    corners(xs.at[1], fs, fr, "send")
    corners(gs.at[1], gsend, grecv, "send")
    for ds in (-1, 1):
        @pl.when(valid(t, s, 0, ds))
        def _(ds=ds):
            cot_row(ds).wait_send()
    for dt in (-1, 1):
        for ds in (-1, 0, 1):
            @pl.when(valid(t, s, dt, ds))
            def _(dt=dt, ds=ds):
                cot_col(dt, ds).wait_send()
    wait_bytes(cw.at[0, :, :, pl.ds(0, 16), :], ws.at[0])
    wait_bytes(cw.at[pl.ds(0, 3), :, :, pl.ds(0, 32), :], ws.at[1])
    for y in range(2):
        forward_cot(y).wait_send()
    for k in range(1, TM):
        give_tile(k).wait_send()
    wait_bytes(pz.at[pl.ds(0, 15)], ps.at[0])

    @pl.when(jnp.logical_and(z == 0, s > 0))
    def _():
        wait_bytes(edges.at[0], ps.at[1])
        wait_bytes(pz.at[pl.ds(0, 6)], ps.at[3])

    @pl.when(jnp.logical_and(z == ZG - 1, s < SPACE - 1))
    def _():
        wait_bytes(edges.at[0], ps.at[2])
        wait_bytes(pz.at[pl.ds(0, 6)], ps.at[4])

    for m in range(3):
        give_pair(m).wait_send()
        wait_bytes(r1.at[m, pl.ds(0, 3)], asend.at[m])
        wait_bytes(r2.at[m, pl.ds(0, 15)], asend.at[3 + m])
    wait_bytes(rb.at[pl.ds(0, 31)], bs)


def shards(features, weight_a, weight_b, cotangent):
    vmem = pl.BlockSpec(memory_space=pltpu.VMEM)
    far = pl.BlockSpec(memory_space=pl.ANY)
    dma = pltpu.SemaphoreType.DMA
    gf, ga, gb = pl.pallas_call(
        body,
        out_shape=(
            jax.ShapeDtypeStruct((2, 4, 128, 128), BF16),
            jax.ShapeDtypeStruct((3, 3, 3, 2, 128), F32),
            jax.ShapeDtypeStruct((3, 3, 3, 2, 512), F32),
        ),
        in_specs=[far, far, far, far],
        out_specs=(vmem, vmem, vmem),
        scratch_shapes=[
            pltpu.VMEM((3456, 256), BF16),
            pltpu.VMEM((27, 256, 512), BF16),
            pltpu.VMEM((3, 4, 6, 128, 128), BF16),
            pltpu.VMEM((3, 6, 4, 16, 512), BF16),
            pltpu.VMEM((4, 4, 2, 64, 128), BF16),
            pltpu.VMEM((2, 16, 512), BF16),
            pltpu.VMEM((2, 3, 16, 512), BF16),
            pltpu.VMEM((2, 3, 16, 512), F32),
            pltpu.VMEM((4, 2, 16, 256), BF16),
            pltpu.VMEM((2, 64, 256), BF16),
            pltpu.VMEM((1024, 256), F32),
            pltpu.VMEM((2, 128, 128), F32),
            pltpu.VMEM((4, 64, 128), BF16),
            pltpu.VMEM((24, 64, 128), BF16),
            pltpu.VMEM((3, 4, 6, 128, 256), BF16),
            pltpu.VMEM((256, 1024), BF16),
            pltpu.VMEM((4, 6, 576, 128), BF16),
            pltpu.VMEM((6912, 128), F32),
            pltpu.VMEM((2048, 128), F32),
            pltpu.VMEM((32, 64, 128), BF16),
            pltpu.VMEM((32, 64, 128), BF16),
            pltpu.VMEM((27, 2, 64, 128), BF16),
            pltpu.VMEM((27, 2, 64, 128), BF16),
            pltpu.VMEM((2, 64, 128), F32),
            pltpu.VMEM((3, 4, 288, 128), BF16),
            pltpu.VMEM((3, 4, 288, 128), BF16),
            pltpu.VMEM((512, 128), F32),
            pltpu.VMEM((3, 16, 32, 128), BF16),
            pltpu.VMEM((3, 16, 32, 128), BF16),
            pltpu.VMEM((2, 16, 512), F32),
            pltpu.VMEM((2, 128, 128), F32),
            pltpu.VMEM((2, 4, 32, 128), BF16),
            pltpu.VMEM((2, 4, 32, 128), BF16),
            pltpu.VMEM((64, 128), F32),
            pltpu.VMEM((4608, 128), BF16),
            pltpu.VMEM((3, 256, 128), F32),
            pltpu.VMEM((6912, 128), BF16),
            dma((5,)), dma((8,)), dma((8,)), dma((8,)), dma((8,)), dma((4,)), dma((4,)),
            dma((3,)), dma((3,)), dma((5,)), dma((3,)), dma((8,)), dma((8,)),
            dma, dma, dma((3,)), dma((3,)), dma((6,)), dma((6,)),
        ],
        compiler_params=pltpu.CompilerParams(collective_id=0, has_side_effects=True, vmem_limit_bytes=56 * 2**20),
    )(features, weight_a.reshape(3456, 256), weight_b.reshape(27, 256, 512), cotangent)
    return (gf, ga.transpose(0, 1, 2, 4, 3), gb)


def solution(mesh):
    placed = (P("tm", "space", None, None), P(), P(), P(None, "space", "tm", None))
    return jax.shard_map(
        shards,
        mesh=mesh,
        in_specs=placed,
        out_specs=(
            P("tm", "space", None, None),
            P(None, None, None, None, ("tm", "space")),
            P(None, None, None, ("tm", "space"), None),
        ),
        check_vma=False,
    )
```

time: 79.8 us -> 63.4 us (0.79)
  Pallas kernels: 73.4 us -> 57.9 us
    pallas_call x1, Pallas kernels: 73.4 us -> 57.9 us  [shards(): pl.pallas_call(body, out_shape=(jax.ShapeDtypeStruct((2, 4, 128, 128), BF...]
    unnamed x1 -> x3, local copies, waits for them, and re-layouts: 1.67 us -> 4.58 us
    transpose x4 -> x0, local copies, waits for them, and re-layouts: 2.38 us -> none  [the longest x2 1.39 us: shards(): ga.reshape(2, 32, 128)[:, :27].transpose(1, 2, 0).reshape(3, 3, 3, 128, 2)]
where the time goes in v2:
time: 63.4 us; the launch traced here: 63.1 us
  Pallas kernels  57.9 us (91%)
  local copies, waits for them, and re-layouts  4.58 us (7%)
  between operations  0.64 us (1%)
    pallas_call x1, Pallas kernels, shards(): pl.pallas_call(body, out_shape=(jax.ShapeDtypeStruct((2, 4, 128, 128), BF...  57.9 us
    unnamed x3, local copies, waits for them, and re-layouts  4.58 us

profile of v2, /device:TPU:1, one launch (start us, length us, event | category | flops | bytes accessed | tf_op | source)
XLA Modules:
  0.0 63.1 jit_solution(8649564083917513891)
XLA Ops:
  0.6 57.9 %shard_map.67 = (bf16[2,4,128,128]{3,2,1,0:T(8,128)(2,1)}, f32[3,3,3,2,128]{4,3,2,1,0:T(2,128)}, f32[3,3,3,2,512]{4,3,2,1,0:T(2,128)}) custom-call(bf16[2,4,128,128]{3,2,1,0:T(8,128)(2,1)} %feat.1, bf16[3456,256]{1,0:T(8,128)(2,1)} %bitcast.4, bf16[27,256,512]{2,1,0:T(8,128)(2,1)} %bitcast.3, bf16[4,2,16,512]{3,2,1,0:T(8,128)(2,1)} %cot.1), custom_call_target="tpu_custom_call" | custom-call | tf_op jit(solution)/shard_map/pallas_call | solution.py:657
  58.5 1.7 %copy.10 = bf16[2,4,128,128]{3,2,1,0:T(8,128)(2,1)} copy(bf16[2,4,128,128]{3,2,1,0:T(8,128)(2,1)} %get-tuple-element.12) | data formatting | bytes 524288
  60.2 1.4 %copy.11 = f32[3,3,3,128,2]{3,4,2,1,0:T(2,128)} copy(f32[3,3,3,128,2]{3,4,2,1,0:T(2,128)} %bitcast.5) | data formatting | bytes 55296
  61.6 1.5 %copy.12 = f32[3,3,3,2,512]{4,3,2,1,0:T(2,128)} copy(f32[3,3,3,2,512]{4,3,2,1,0:T(2,128)} %get-tuple-element.14) | data formatting | bytes 221184

commit v3 on v2

--- a/solution.py
+++ b/solution.py
@@ -445,21 +445,20 @@
         taps = pl.ds(m * 9, 9)
         return remote(pxs.at[taps], pxr.at[taps], xsend.at[m], xrecv.at[m], partner, s)
 
-    def term(ab, carry):
-        a, b = (ab // 3, lax.rem(ab, 3))
-        rhs = jnp.concatenate([xs[c, pl.ds(a, 2), pl.ds(b, 4)].reshape(1024, 128) for c in range(3)], axis=1)
-        res = dot(gt[...], rhs)
-        for c in range(3):
-            n = ab * 3 + c
-            base = n * 256
-            outa[pl.ds(pl.multiple_of(base, 256), 256), :] = res[:, c * 128 : c * 128 + 128]
+    for m in range(3):
+        rhs = [xs[c, pl.ds(m, 2), pl.ds(b, 4)].reshape(1024, 128) for b in range(3) for c in range(3)]
+        res = dot(gt[...], jnp.concatenate(rhs, axis=1))
+        for k in range(9):
+            outa[pl.ds((m * 9 + k) * 256, 256), :] = res[:, k * 128 : k * 128 + 128]
+
+        def cut_a(k, carry, m=m):
+            n = m * 9 + k
             for y in range(2):
-                other = pl.multiple_of(base + (1 - core + 2 * y) * 64, 64)
+                other = pl.multiple_of(n * 256 + (1 - core + 2 * y) * 64, 64)
                 pxs[n, y] = outa[pl.ds(other, 64), :].astype(BF16)
-        return carry
-
-    for m in range(3):
-        lax.fori_loop(m * 3, m * 3 + 3, term, 0)
+            return carry
+
+        lax.fori_loop(0, 9, cut_a, 0)
         give_pair(m).start()
     halo_wait(gs.at[1], gs.at[1], 1, (2, 3), gsend, grecv)
     corners(gs.at[1], gsend, grecv, "start")

time: 63.4 us -> 62.1 us (0.979)
  Pallas kernels: 57.9 us -> 56.7 us
    pallas_call x1, Pallas kernels: 57.9 us -> 56.7 us  [shards(): pl.pallas_call(body, out_shape=(jax.ShapeDtypeStruct((2, 4, 128, 128), BF...]
where the time goes in v3:
time: 62.1 us; the launch traced here: 61.9 us
  Pallas kernels  56.7 us (91%)
  local copies, waits for them, and re-layouts  4.58 us (7%)
  between operations  0.64 us (1%)
    pallas_call x1, Pallas kernels, shards(): pl.pallas_call(body, out_shape=(jax.ShapeDtypeStruct((2, 4, 128, 128), BF...  56.7 us
    unnamed x3, local copies, waits for them, and re-layouts  4.58 us

profile of v3, /device:TPU:1, one launch (start us, length us, event | category | flops | bytes accessed | tf_op | source)
XLA Modules:
  0.0 61.9 jit_solution(12268617091602871024)
XLA Ops:
  0.6 56.7 %shard_map.67 = (bf16[2,4,128,128]{3,2,1,0:T(8,128)(2,1)}, f32[3,3,3,2,128]{4,3,2,1,0:T(2,128)}, f32[3,3,3,2,512]{4,3,2,1,0:T(2,128)}) custom-call(bf16[2,4,128,128]{3,2,1,0:T(8,128)(2,1)} %feat.1, bf16[3456,256]{1,0:T(8,128)(2,1)} %bitcast.4, bf16[27,256,512]{2,1,0:T(8,128)(2,1)} %bitcast.3, bf16[4,2,16,512]{3,2,1,0:T(8,128)(2,1)} %cot.1), custom_call_target="tpu_custom_call" | custom-call | tf_op jit(solution)/shard_map/pallas_call | solution.py:656
  57.3 1.7 %copy.10 = bf16[2,4,128,128]{3,2,1,0:T(8,128)(2,1)} copy(bf16[2,4,128,128]{3,2,1,0:T(8,128)(2,1)} %get-tuple-element.12) | data formatting | bytes 524288
  59.0 1.4 %copy.11 = f32[3,3,3,128,2]{3,4,2,1,0:T(2,128)} copy(f32[3,3,3,128,2]{3,4,2,1,0:T(2,128)} %bitcast.5) | data formatting | bytes 55296
  60.3 1.5 %copy.12 = f32[3,3,3,2,512]{4,3,2,1,0:T(2,128)} copy(f32[3,3,3,2,512]{4,3,2,1,0:T(2,128)} %get-tuple-element.14) | data formatting | bytes 221184

commit v4 on v3

--- a/solution.py
+++ b/solution.py
@@ -207,11 +207,6 @@
                 else:
                     copy.wait_send()
 
-    for d in range(4):
-        @pl.when(valid(t, s, *SIDES[d]))
-        def _(d=d):
-            halo_copy(feat, xs.at[1], 0, d, fs, fr).start()
-
     def cot_row(ds):
         r0, _ = source_span(ds, 2)
         lr, _ = landing_span(ds, 2)
@@ -247,6 +242,11 @@
             @pl.when(valid(t, s, dt, ds))
             def _(dt=dt, ds=ds):
                 cot_col(dt, ds).start()
+
+    for d in range(4):
+        @pl.when(valid(t, s, *SIDES[d]))
+        def _(d=d):
+            halo_copy(feat, xs.at[1], 0, d, fs, fr).start()
 
     def gather_cot(j, tt, zd):
         return remote(
@@ -433,14 +433,6 @@
     def pass_edge(k, zd):
         return remote(edges.at[k], edges.at[k], ps.at[3 + k], pr.at[1 + k], t, group + zd)
 
-    for k, passes in ((0, jnp.logical_and(z == 0, s > 0)), (1, jnp.logical_and(z == ZG - 1, s < SPACE - 1))):
-        @pl.when(passes)
-        def _(k=k):
-            wait_bytes(edges.at[k], pr.at[1 + k])
-            for j in range(1, ZG):
-                pass_edge(k, lax.rem(z + j, ZG)).start()
-
-
     def give_pair(m):
         taps = pl.ds(m * 9, 9)
         return remote(pxs.at[taps], pxr.at[taps], xsend.at[m], xrecv.at[m], partner, s)
@@ -460,6 +452,14 @@
 
         lax.fori_loop(0, 9, cut_a, 0)
         give_pair(m).start()
+        if m == 1:
+            for k, passes in ((0, jnp.logical_and(z == 0, s > 0)), (1, jnp.logical_and(z == ZG - 1, s < SPACE - 1))):
+                @pl.when(passes)
+                def _(k=k):
+                    wait_bytes(edges.at[k], pr.at[1 + k])
+                    for j in range(1, ZG):
+                        pass_edge(k, lax.rem(z + j, ZG)).start()
+
     halo_wait(gs.at[1], gs.at[1], 1, (2, 3), gsend, grecv)
     corners(gs.at[1], gsend, grecv, "start")
     fill_shifts(gs, True)

time: 62.1 us -> 60.6 us (0.976)
  Pallas kernels: 56.7 us -> 55.2 us
    pallas_call x1, Pallas kernels: 56.7 us -> 55.2 us  [shards(): pl.pallas_call(body, out_shape=(jax.ShapeDtypeStruct((2, 4, 128, 128), BF...]
where the time goes in v4:
time: 60.6 us; the launch traced here: 60.4 us
  Pallas kernels  55.2 us (91%)
  local copies, waits for them, and re-layouts  4.58 us (8%)
  between operations  0.64 us (1%)
    pallas_call x1, Pallas kernels, shards(): pl.pallas_call(body, out_shape=(jax.ShapeDtypeStruct((2, 4, 128, 128), BF...  55.2 us
    unnamed x3, local copies, waits for them, and re-layouts  4.58 us

profile of v4, /device:TPU:1, one launch (start us, length us, event | category | flops | bytes accessed | tf_op | source)
XLA Modules:
  0.0 60.4 jit_solution(15072622648667178195)
XLA Ops:
  0.6 55.2 %shard_map.67 = (bf16[2,4,128,128]{3,2,1,0:T(8,128)(2,1)}, f32[3,3,3,2,128]{4,3,2,1,0:T(2,128)}, f32[3,3,3,2,512]{4,3,2,1,0:T(2,128)}) custom-call(bf16[2,4,128,128]{3,2,1,0:T(8,128)(2,1)} %feat.1, bf16[3456,256]{1,0:T(8,128)(2,1)} %bitcast.4, bf16[27,256,512]{2,1,0:T(8,128)(2,1)} %bitcast.3, bf16[4,2,16,512]{3,2,1,0:T(8,128)(2,1)} %cot.1), custom_call_target="tpu_custom_call" | custom-call | tf_op jit(solution)/shard_map/pallas_call | solution.py:656
  55.8 1.7 %copy.10 = bf16[2,4,128,128]{3,2,1,0:T(8,128)(2,1)} copy(bf16[2,4,128,128]{3,2,1,0:T(8,128)(2,1)} %get-tuple-element.12) | data formatting | bytes 524288
  57.5 1.4 %copy.11 = f32[3,3,3,128,2]{3,4,2,1,0:T(2,128)} copy(f32[3,3,3,128,2]{3,4,2,1,0:T(2,128)} %bitcast.5) | data formatting | bytes 55296
  58.8 1.5 %copy.12 = f32[3,3,3,2,512]{4,3,2,1,0:T(2,128)} copy(f32[3,3,3,2,512]{4,3,2,1,0:T(2,128)} %get-tuple-element.14) | data formatting | bytes 221184

commit v5 on v4

--- a/solution.py
+++ b/solution.py
@@ -304,8 +304,6 @@
         zz[k, 5] = jnp.zeros(zz.shape[2:], BF16)
 
     load_wa.wait()
-    for n in range(27):
-        wt[pl.ds(n * 256, 256), :] = wa[pl.ds(n * 128, 128), :].astype(F32).T.astype(BF16)
     keep_feat.wait()
     fill_shifts(xs, True)
     for ds in (-1, 1):
@@ -581,6 +579,8 @@
     for m in range(3):
         second(m)
 
+    for n in range(27):
+        wt[pl.ds(n * 256, 256), :] = wa[pl.ds(n * 128, 128), :].astype(F32).T.astype(BF16)
     halo_wait(gs.at[1], gs.at[1], 1, (0, 1), gsend, grecv)
     corners(gs.at[1], gsend, grecv, "recv")
     fill_shifts(gs, False)

time: 60.6 us -> 60.6 us (level)
  no operation moved by 1% of the time
where the time goes in v5:
time: 60.6 us; the launch traced here: 60.4 us
  Pallas kernels  55.2 us (91%)
  local copies, waits for them, and re-layouts  4.58 us (8%)
  between operations  0.64 us (1%)
    pallas_call x1, Pallas kernels, shards(): pl.pallas_call(body, out_shape=(jax.ShapeDtypeStruct((2, 4, 128, 128), BF...  55.2 us
    unnamed x3, local copies, waits for them, and re-layouts  4.58 us

profile of v5, /device:TPU:1, one launch (start us, length us, event | category | flops | bytes accessed | tf_op | source)
XLA Modules:
  0.0 60.4 jit_solution(9888966895348934924)
XLA Ops:
  0.6 55.2 %shard_map.67 = (bf16[2,4,128,128]{3,2,1,0:T(8,128)(2,1)}, f32[3,3,3,2,128]{4,3,2,1,0:T(2,128)}, f32[3,3,3,2,512]{4,3,2,1,0:T(2,128)}) custom-call(bf16[2,4,128,128]{3,2,1,0:T(8,128)(2,1)} %feat.1, bf16[3456,256]{1,0:T(8,128)(2,1)} %bitcast.4, bf16[27,256,512]{2,1,0:T(8,128)(2,1)} %bitcast.3, bf16[4,2,16,512]{3,2,1,0:T(8,128)(2,1)} %cot.1), custom_call_target="tpu_custom_call" | custom-call | tf_op jit(solution)/shard_map/pallas_call | solution.py:656
  55.8 1.7 %copy.10 = bf16[2,4,128,128]{3,2,1,0:T(8,128)(2,1)} copy(bf16[2,4,128,128]{3,2,1,0:T(8,128)(2,1)} %get-tuple-element.12) | data formatting | bytes 524288
  57.5 1.4 %copy.11 = f32[3,3,3,128,2]{3,4,2,1,0:T(2,128)} copy(f32[3,3,3,128,2]{3,4,2,1,0:T(2,128)} %bitcast.5) | data formatting | bytes 55296
  58.8 1.5 %copy.12 = f32[3,3,3,2,512]{4,3,2,1,0:T(2,128)} copy(f32[3,3,3,2,512]{4,3,2,1,0:T(2,128)} %get-tuple-element.14) | data formatting | bytes 221184
